TPU v7x, 1024 devices: a whole 8x8x8 slice. The times are simulated.
1024 devices in a mesh: gy: 8 (over y), gx: 128 (over x, z, core).
Axes of the slice: x: 8, y: 8, z: 8, core: 2. Of those that a mesh axis runs over, the one named last changes fastest.
Arguments:
- cotangent: float32 [3, 64, 2048, 256], P(None, 'gy', 'gx'), may hold values from -8 to 8
- coefficient: float32 [64, 2048, 256], P('gy', 'gx'), may hold values from 0.05 to 4
Outputs:
- velocity_grad: float32 [3, 64, 2048, 256], P(None, 'gy', 'gx')
- adjoint_pressure: float32 [64, 2048, 256], P('gy', 'gx')
All inputs are finite; a program needn't handle non-finite values.
Results may differ from a plain program's by a relative error of at most 0.0025.
Values sent between devices are 32-bit elements; how exact they have to be, the bound alone decides.
No kernel may reach another device: no remote copies, remote signals or barrier semaphores. Data moves between devices by JAX's collectives and lax.ppermute only.
A program may use at most 32 MiB of HBM per device.

v0:
```python
import jax
import jax.numpy as jnp
from jax import lax
from jax.sharding import PartitionSpec as P

ITERS = 4


def with_halo(x, sides, width):
    for axis, dim in sides:
        size, length = (lax.axis_size(axis), x.shape[dim])
        up = [(i, (i + 1) % size) for i in range(size - 1)]
        down = [(j, i) for i, j in up]
        last = lax.slice_in_dim(x, length - width, length, axis=dim)
        initial = lax.slice_in_dim(x, 0, width, axis=dim)
        before = lax.ppermute(last, axis, up)
        after = lax.ppermute(initial, axis, down)
        x = jnp.concatenate([before, x, after], axis=dim)
    return x


def pad_faces(field):
    return with_halo(field, (("gy", 1), ("gx", 2)), 1)


def global_sum(values):
    partial_rows = lax.psum((values[0],), "gx")
    return lax.psum((partial_rows[0],), "gy")


def pad_depth(center):
    return jnp.pad(center, ((0, 0), (0, 0), (0, 0), (1, 1)))


def operate_on(padded, scaling):
    center = padded[:, 1:-1, 1:-1, :]
    beside = padded[:, :-2, 1:-1, :] + padded[:, 2:, 1:-1, :]
    beside = beside + padded[:, 1:-1, :-2, :] + padded[:, 1:-1, 2:, :]
    deeper = pad_depth(center)
    beside = beside + deeper[..., :-2] + deeper[..., 2:]
    return scaling * center - beside


def on_device(cotangent, coefficient):
    padded_grad = pad_faces(cotangent[0:2])
    depth_grad = pad_depth(cotangent[2:3])
    source = (
        padded_grad[0:1, :-2, 1:-1, :]
        - cotangent[0:1]
        + (padded_grad[1:2, 1:-1, :-2, :] - cotangent[1:2])
        + (depth_grad[..., :-2] - cotangent[2:3])
    )
    scaling = 6.0 + coefficient[None]
    residual = source
    precond = residual / scaling
    adjoint_pad = jnp.zeros(
        (1, scaling.shape[1] + 2, scaling.shape[2] + 2, scaling.shape[3]), jnp.float32
    )
    direction = precond
    energy = global_sum((jnp.sum(residual * precond),))[0]
    for sweep in range(ITERS):
        padded_dir = pad_faces(direction)
        image = operate_on(padded_dir, scaling)
        step_size = energy / global_sum((jnp.sum(direction * image),))[0]
        adjoint_pad = adjoint_pad + step_size * padded_dir
        if sweep + 1 < ITERS:
            residual = residual - step_size * image
            precond = residual / scaling
            fresh = global_sum((jnp.sum(residual * precond),))[0]
            direction = precond + fresh / energy * direction
            energy = fresh
    adjoint = adjoint_pad[:, 1:-1, 1:-1, :]
    adjoint_pad = pad_faces(adjoint)
    depth_adj = pad_depth(adjoint)
    velocity = jnp.concatenate(
        [
            cotangent[0:1] + adjoint_pad[:, 2:, 1:-1, :] - adjoint,
            cotangent[1:2] + adjoint_pad[:, 1:-1, 2:, :] - adjoint,
            cotangent[2:3] + depth_adj[..., 2:] - adjoint,
        ],
        axis=0,
    )
    return (velocity, adjoint[0])


def solution(mesh):
    return jax.shard_map(
        on_device,
        mesh=mesh,
        in_specs=(P(None, "gy", "gx", None), P("gy", "gx", None)),
        out_specs=(P(None, "gy", "gx", None), P("gy", "gx", None)),
        check_vma=False,
    )
```

profile of v0, /device:TPU:1, one launch (start us, length us, event | category | flops | bytes accessed | tf_op | source)
XLA Modules:
  0.0 1964.1 jit_solution(8946347339416924691)
XLA Ops:
  1.4 4.1 collective-permute-start
  10.3 7.0 collective-permute-start.2
  17.3 7.5 collective-permute-done.2
  27.6 3.2 collective-permute-done.4
  38.5 256.4 %all-reduce.6 = (f32[]{:T(128)}, f32[]{:T(128)}) all-reduce(f32[]{:T(128)} %get-tuple-element.3, f32[]{:T(128)} %get-tuple-element.2), channel_id=1, replica_groups=mesh['gy'=8,'gx'=128] {'gx'}, use_global_device_ids=true, to_apply=%region_1.2 | all-reduce | flops 2 | bytes 16 | tf_op jit(solution)/shard_map/psum | solution.py:27
  294.8 14.6 all-reduce.7
  311.4 253.6 %psum.116 = f32[]{:T(128)} all-reduce(f32[]{:T(128)} %get-tuple-element.14), channel_id=1, replica_groups=mesh['gy'=8,'gx'=128] {'gx'}, use_global_device_ids=true, to_apply=%region_7.8 | all-reduce | flops 1 | bytes 8 | tf_op jit(solution)/shard_map/psum | solution.py:27
  565.0 11.8 psum.117
  578.2 3.3 collective-permute-start.7
  582.8 3.2 collective-permute-done.8
  586.0 3.4 collective-permute-start.9
  589.3 5.2 collective-permute-start.10
  596.1 247.1 %psum.118 = f32[]{:T(128)} all-reduce(f32[]{:T(128)} %get-tuple-element.12), channel_id=1, replica_groups=mesh['gy'=8,'gx'=128] {'gx'}, use_global_device_ids=true, to_apply=%region_10.11 | all-reduce | flops 1 | bytes 8 | tf_op jit(solution)/shard_map/psum | solution.py:27
  843.3 13.6 psum.119
  858.8 251.2 %psum.120 = f32[]{:T(128)} all-reduce(f32[]{:T(128)} %get-tuple-element.10), channel_id=1, replica_groups=mesh['gy'=8,'gx'=128] {'gx'}, use_global_device_ids=true, to_apply=%region_13.14 | all-reduce | flops 1 | bytes 8 | tf_op jit(solution)/shard_map/psum | solution.py:27
  1110.0 11.8 psum.121
  1123.2 3.3 collective-permute-start.11
  1127.8 3.2 collective-permute-done.12
  1131.0 3.4 collective-permute-start.13
  1134.4 5.2 collective-permute-start.14
  1141.2 247.1 %psum.122 = f32[]{:T(128)} all-reduce(f32[]{:T(128)} %get-tuple-element.8), channel_id=1, replica_groups=mesh['gy'=8,'gx'=128] {'gx'}, use_global_device_ids=true, to_apply=%region_16.17 | all-reduce | flops 1 | bytes 8 | tf_op jit(solution)/shard_map/psum | solution.py:27
  1388.3 13.6 psum.123
  1403.9 251.2 %psum.124 = f32[]{:T(128)} all-reduce(f32[]{:T(128)} %multiply_reduce_fusion), channel_id=1, replica_groups=mesh['gy'=8,'gx'=128] {'gx'}, use_global_device_ids=true, to_apply=%region_19.20 | all-reduce | flops 1 | bytes 8 | tf_op jit(solution)/shard_map/psum | solution.py:27
  1655.1 11.8 psum.125
  1668.3 3.3 collective-permute-start.15
  1672.9 3.2 collective-permute-done.16
  1676.1 3.4 collective-permute-start.17
  1679.5 5.2 collective-permute-start.18
  1686.3 247.1 %psum.126 = f32[]{:T(128)} all-reduce(f32[]{:T(128)} %fusion.20), channel_id=1, replica_groups=mesh['gy'=8,'gx'=128] {'gx'}, use_global_device_ids=true, to_apply=%region_22.23 | all-reduce | flops 1 | bytes 8 | tf_op jit(solution)/shard_map/psum | solution.py:27
  1933.4 13.6 psum.127
  1952.1 2.9 collective-permute-done.19
  1955.0 7.5 collective-permute-start.21
  (60 shorter events, 31.9 us)
Async XLA Ops:
  1.4 6.5 collective-permute-start
  5.6 4.7 collective-permute-start.1
  6.9 18.0 copy-start.1
  10.2 14.6 copy-start
  10.3 14.6 slice-start
  10.3 14.5 collective-permute-start.2
  25.0 2.6 collective-permute-start.3
  26.3 4.5 collective-permute-start.4
  30.8 4.8 collective-permute-start.5
  32.7 5.0 collective-permute-start.6
  578.2 4.6 collective-permute-start.7
  581.5 4.5 collective-permute-start.8
  586.0 8.6 collective-permute-start.9
  589.3 6.1 collective-permute-start.10
  1123.2 4.6 collective-permute-start.11
  1126.5 4.5 collective-permute-start.12
  1131.0 8.6 collective-permute-start.13
  1134.4 6.1 collective-permute-start.14
  1668.3 4.6 collective-permute-start.15
  1671.6 4.5 collective-permute-start.16
  1676.1 8.6 collective-permute-start.17
  1679.5 6.1 collective-permute-start.18
  1948.5 3.5 collective-permute-start.20
  1950.1 4.9 collective-permute-start.19
  1955.0 8.3 collective-permute-start.21
where the time goes:
time: 2000 us; the launch traced here: 1960 us
  blocking collectives  1840 us (92%)
  starting transfers between devices  69.7 us (3%)
  waiting for transfers between devices  30.7 us (2%)
    psum x7, blocking collectives, global_sum(): partial_rows = lax.psum((values[0],), 'gx')  1750 us
    psum x7, blocking collectives, global_sum(): return lax.psum((partial_rows[0],), 'gy')  90.8 us
  transfers between devices with their start and end apart: 22, of which 12 were waited for; matrix products, arithmetic and copies ran while one was open for 0% of the time, Pallas kernels for 0%

commit v1 on v0

v1 whole, which is shorter than its diff:
```python
import functools

import jax
import jax.numpy as jnp
import numpy as np
from jax import lax
from jax.experimental import pallas as pl
from jax.experimental.pallas import tpu as pltpu
from jax.sharding import Mesh, PartitionSpec as P

ITERS = 4
HALO = ITERS
SHIFTS = (0.25, 1.0)
SPLIT = 0.6
NMOM = 2 * ITERS
AXES = ("y", "xh", "xl", "z", "c")
STAGE = (("xh", "z", "c"), ("y", "xl"))
F32 = jnp.float32


def iota(shape, axis):
    return lax.broadcasted_iota(jnp.int32, shape, axis)


def pack_kernel(cot, coef, t_out, d_out, up, down, right, left, up_r, up_l, down_r, down_l):
    ny, nx, nz = coef.shape
    sub, lane = iota((nx, nz), 0), iota((nx, nz), 1)
    sub8 = iota((8, nz), 0)
    column = jnp.zeros((8, nz), F32)
    for y in range(ny):
        c0, c1, c2 = cot[0, y], cot[1, y], cot[2, y]
        d = 1.0 / (6.0 + coef[y])
        t = jnp.where(sub == 0, 0.0, pltpu.roll(c1, 1, 0)) - c1
        t = t + (jnp.where(lane == 0, 0.0, pltpu.roll(c2, 1, 1)) - c2)
        t = t + ((cot[0, y - 1] - c0) if y else -c0)
        t_out[y] = t
        d_out[y] = d
        to_right = jnp.where(sub8 >= 4, t[nx - 8 :], pltpu.roll(d[nx - 8 :], 4, 0))
        to_left = jnp.where(sub8 < 4, t[:8], pltpu.roll(d[:8], 4, 0))
        right[y] = to_right
        left[y] = to_left
        if y < HALO:
            down[y], down[HALO + y] = t, d
            down_r[y], down_l[y] = to_right, to_left
        if y >= ny - HALO:
            j = y - (ny - HALO)
            up[j], up[HALO + j] = t, d
            up_r[j], up_l[j] = to_right, to_left
        column = jnp.where(sub8 == y, jnp.broadcast_to(c1[nx - 1 : nx], (8, nz)), column)
    edge = cot[0, ny - 1]
    up[2 * HALO] = edge
    right[ny] = edge[nx - 8 :]
    left[ny] = edge[:8]
    up_r[HALO] = edge[nx - 8 :]
    up_l[HALO] = edge[:8]
    right[ny + 1] = column
    up_r[HALO + 1] = column
    down_r[HALO] = column
    wide = jnp.concatenate([column, jnp.zeros((nx - 8, nz), F32)], axis=0)
    up[2 * HALO + 1] = wide
    down[2 * HALO] = wide


def krylov_kernel(t_own, d_own, coef, up, right, r_s, r_n, r_l, r_r, r_sw, r_se, r_nw, r_ne, v, part, dw):
    ny, nx, nz = coef.shape
    sub8 = iota((8, nz), 0)
    lane = iota((nx + 8, nz), 1)
    low = sub8 < 4

    def at_first(col_ref_value, k):
        return jnp.where(sub8 == 0, jnp.broadcast_to(col_ref_value[k : k + 1], (8, nz)), 0.0)

    def assemble(row, t, d, from_left, from_right, edge, edge_side, col_low, col_high, k):
        t_side = jnp.where(low, from_right, from_left)
        d_side = pltpu.roll(jnp.where(low, from_left, from_right), 4, 0)
        if edge is not None:
            t = t + edge
            t_side = t_side + edge_side
        t_first = t[:8] + at_first(col_low, k)
        t_side = t_side + at_first(col_high, k)
        v[0, row, 0:8] = t_first * d[:8]
        v[0, row, 8:nx] = t[8:] * d[8:]
        v[0, row, nx : nx + 8] = t_side * d_side
        dw[row, 0:nx] = d
        dw[row, nx : nx + 8] = d_side

    own_low, own_high = r_l[ny + 1], right[ny + 1]
    for y in range(ny):
        edge = edge_side = None
        if y == 0:
            edge = r_s[2 * HALO]
            edge_side = jnp.where(low, r_se[HALO], r_sw[HALO])
        assemble(y, t_own[y], d_own[y], r_l[y], r_r[y], edge, edge_side, own_low, own_high, y)
    col_low, col_high = r_nw[HALO], r_n[2 * HALO][:8]
    for j in range(HALO):
        edge = edge_side = None
        if j == 0:
            edge = up[2 * HALO]
            edge_side = jnp.where(low, r_r[ny], r_l[ny])
        assemble(ny + j, r_n[j], r_n[HALO + j], r_nw[j], r_ne[j], edge, edge_side, col_low, col_high, j)
    col_low, col_high = r_sw[HALO + 1], r_s[2 * HALO + 1][:8]
    for j in range(HALO):
        assemble(
            ny + HALO + j, r_s[j], r_s[HALO + j], r_sw[j], r_se[j], None, None, col_low, col_high, ny - HALO + j
        )

    rows = ny + 2 * HALO

    def powered(k, row):
        row = row % rows
        x = v[k, row]
        beside = v[k, (row + 1) % rows] + v[k, (row - 1) % rows]
        beside = beside + (pltpu.roll(x, 1, 0) + pltpu.roll(x, nx + 7, 0))
        beside = beside + jnp.where(lane == 0, 0.0, pltpu.roll(x, 1, 1))
        beside = beside + jnp.where(lane == nz - 1, 0.0, pltpu.roll(x, nz - 1, 1))
        return x - dw[row] * beside

    for k in range(ITERS - 1):
        reach = HALO - 1 - k
        for row in range(-reach, ny + reach):
            v[k + 1, row % rows] = powered(k, row)
    total = [jnp.zeros((8, 128), F32) for _ in range(NMOM * len(SHIFTS))]
    for y in range(ny):
        scaling = 6.0 + coef[y]
        last = powered(ITERS - 1, y)
        for a in range(0, nx, 8):
            for b in range(0, nz, 128):
                m = scaling[a : a + 8, b : b + 128]
                base = [v[k, y, a : a + 8, b : b + 128] for k in range(ITERS)] + [last[a : a + 8, b : b + 128]]
                for i, mu in enumerate(SHIFTS):
                    level, shifted = base, [base[0]]
                    for _ in range(ITERS):
                        level = [hi - (lo if mu == 1.0 else mu * lo) for lo, hi in zip(level, level[1:])]
                        shifted.append(level[0])
                    for k in range(ITERS):
                        weighted = m * shifted[k]
                        n = i * NMOM + 2 * k
                        total[n] = total[n] + weighted * shifted[k]
                        total[n + 1] = total[n + 1] + weighted * shifted[k + 1]
    stacked = jnp.concatenate([jnp.sum(x, axis=0, keepdims=True) for x in total], axis=0)
    sums = jnp.sum(stacked, axis=1, keepdims=True)
    n = len(total)
    diagonal = iota((n, 128), 0) == iota((n, 128), 1)
    line = jnp.sum(jnp.where(diagonal, sums, 0.0), axis=0, keepdims=True)
    part[...] = jnp.broadcast_to(line[None], part.shape)


def coefficients(moments):
    nearer = moments[1] + (SHIFTS[0] - SPLIT) * moments[0] < 0.0
    mom = [jnp.where(nearer, a, b) for a, b in zip(moments[:NMOM], moments[NMOM:])]
    mu = jnp.where(nearer, SHIFTS[0], SHIFTS[1]).astype(F32)
    zero = jnp.zeros_like(mom[0])
    one = zero + 1.0

    def times(poly):
        return [(lo + mu * hi) for lo, hi in zip([zero] + poly, poly + [zero])]

    sigma, tau = mom, mom
    rho, pi, x = [one], [one], [zero] * ITERS
    energy, lead = mom[0], one
    for k in range(ITERS):
        image = [hi + mu * lo for lo, hi in zip(tau, tau[1:])]
        step = energy / (lead * image[k])
        step = jnp.where((step > 0.4) & (step < 200.0), step, 0.0)
        x = [a + step * b for a, b in zip(x, pi + [zero] * (ITERS - len(pi)))]
        if k + 1 < ITERS:
            sigma = [a - step * b for a, b in zip(sigma, image)]
            rho = [a - step * b for a, b in zip(rho + [zero], times(pi))]
            lead = lead * -step
            fresh = lead * sigma[k + 1]
            fresh = jnp.maximum(fresh, 0.0)
            grow = jnp.where(energy > 0.0, fresh / energy, 0.0)
            tau = [a + grow * b for a, b in zip(sigma, tau)]
            pi = [a + grow * b for a, b in zip(rho, pi + [zero])]
            energy = fresh
    for i in range(ITERS - 1):
        for j in range(ITERS - 2, i - 1, -1):
            x[j] = x[j] - mu * x[j + 1]
    return x


def finish_kernel(parts, v, cot, vel, adj):
    _, ny, nx, nz = cot.shape
    line = jnp.sum(parts[...], axis=0)
    spread = jnp.broadcast_to(line, (8, 128))
    lane = iota((8, 128), 1)
    moments = [
        jnp.sum(jnp.where(lane == n, spread, 0.0), axis=1, keepdims=True) for n in range(NMOM * len(SHIFTS))
    ]
    coef = [c[:1] for c in coefficients(moments)]
    lane = iota((nx, nz), 1)

    def pressure(row):
        total = coef[0] * v[0, row]
        for k in range(1, ITERS):
            total = total + coef[k] * v[k, row]
        return total

    here = pressure(0)
    for y in range(ny):
        above = pressure(y + 1)
        x = here[:nx]
        adj[y] = x
        vel[0, y] = cot[0, y] + above[:nx] - x
        vel[1, y] = cot[1, y] + pltpu.roll(here, nx + 7, 0)[:nx] - x
        vel[2, y] = cot[2, y] + jnp.where(lane == nz - 1, 0.0, pltpu.roll(x, nz - 1, 1)) - x
        here = above


def neighbour(x, dy, dx, ny, nx):
    pairs = [
        (a * nx + b, (a + dy) * nx + b + dx)
        for a in range(ny)
        for b in range(nx)
        if 0 <= a + dy < ny and 0 <= b + dx < nx
    ]
    return lax.ppermute(x, AXES, pairs)


def exchange_sum(x, axes):
    return jnp.sum(lax.all_to_all(x, axes, 0, 0), axis=0, keepdims=True)


def on_device(gy, gx, sizes, cotangent, coefficient):
    ny, nx, nz = coefficient.shape
    block = (ny, nx, nz)
    shapes = [
        block,
        block,
        (2 * HALO + 2, nx, nz),
        (2 * HALO + 1, nx, nz),
        (ny + 2, 8, nz),
        (ny + 1, 8, nz),
        (HALO + 2, 8, nz),
        (HALO + 1, 8, nz),
        (HALO + 1, 8, nz),
        (HALO, 8, nz),
    ]
    limit = pltpu.CompilerParams(vmem_limit_bytes=24 * 1024 * 1024)
    t, d, up, down, right, left, up_r, up_l, down_r, down_l = pl.pallas_call(
        pack_kernel,
        out_shape=[jax.ShapeDtypeStruct(s, F32) for s in shapes],
        compiler_params=limit,
        name="pack",
    )(cotangent, coefficient)
    send = functools.partial(neighbour, ny=gy, nx=gx)
    r_sw = send(up_r, 1, 1)
    r_se = send(up_l, 1, -1)
    r_nw = send(down_r, -1, 1)
    r_ne = send(down_l, -1, -1)
    r_s = send(up, 1, 0)
    r_n = send(down, -1, 0)
    r_l = send(right, 0, 1)
    r_r = send(left, 0, -1)
    first, second = (int(np.prod([sizes[a] for a in axes])) for axes in STAGE)
    rows, wide = ny + 2 * HALO, nx + 8
    v, part = pl.pallas_call(
        krylov_kernel,
        out_shape=[
            jax.ShapeDtypeStruct((ITERS, rows, wide, nz), F32),
            jax.ShapeDtypeStruct((first, 1, 128), F32),
        ],
        scratch_shapes=[pltpu.VMEM((rows, wide, nz), F32)],
        compiler_params=limit,
        name="krylov",
    )(t, d, coefficient, up, right, r_s, r_n, r_l, r_r, r_sw, r_se, r_nw, r_ne)
    part = exchange_sum(part, STAGE[0])
    part = lax.all_to_all(jnp.broadcast_to(part, (second, 1, 128)), STAGE[1], 0, 0)
    return tuple(
        pl.pallas_call(
            finish_kernel,
            out_shape=[
                jax.ShapeDtypeStruct(cotangent.shape, F32),
                jax.ShapeDtypeStruct(coefficient.shape, F32),
            ],
            compiler_params=limit,
            name="finish",
        )(part, v, cotangent)
    )


def solution(mesh):
    gy, gx = mesh.shape["gy"], mesh.shape["gx"]
    fine = Mesh(np.asarray(mesh.devices).reshape(gy, 2, gx // 32, 8, 2), AXES)
    along_x = AXES[1:]
    wide, flat = P(None, AXES[0], along_x, None), P(AXES[0], along_x, None)
    return jax.shard_map(
        functools.partial(on_device, gy, gx, dict(fine.shape)),
        mesh=fine,
        in_specs=(wide, flat),
        out_specs=(wide, flat),
        check_vma=False,
    )
```

time: 2000 us -> 93 us (0.05); the launches traced: 1960 us -> 92.5 us
  blocking collectives: 1840 us -> 50.7 us
  starting transfers between devices: 69.7 us -> 31.3 us
  waiting for transfers between devices: 30.7 us -> 4.71 us
    psum x14 -> x0, blocking collectives: 1840 us -> none  [the longest x7 1750 us: global_sum(): partial_rows = lax.psum((values[0],), 'gx')]
    all_to_all x0 -> x2, blocking collectives: none -> 50.7 us  [the longest x1 28.1 us: exchange_sum(): return jnp.sum(lax.all_to_all(x, axes, 0, 0), axis=0, keepdims=True)]
    ppermute x22 -> x8, starting transfers between devices: 69.7 us -> 31.3 us  [neighbour(): return lax.ppermute(x, AXES, pairs)]
    ppermute x22 -> x8, waiting for transfers between devices: 30.7 us -> 4.71 us  [neighbour(): return lax.ppermute(x, AXES, pairs)]
  transfers between devices with their start and end apart: 22 -> 8, of which waited for: 12 -> 2; matrix products, arithmetic and copies ran while one was open for 0% -> 0% of each run, Pallas kernels for 0% -> 0%
where the time goes in v1:
time: 93 us; the launch traced here: 92.5 us
  blocking collectives  50.7 us (55%)
  starting transfers between devices  31.3 us (34%)
  waiting for transfers between devices  4.71 us (5%)
  local copies, waits for them, and re-layouts  2.81 us (3%)
  Pallas kernels  2.24 us (2%)
    ppermute x8, starting transfers between devices, neighbour(): return lax.ppermute(x, AXES, pairs)  31.3 us
    all_to_all x1, blocking collectives, exchange_sum(): return jnp.sum(lax.all_to_all(x, axes, 0, 0), axis=0, keepdims=True)  28.1 us
    all_to_all x1, blocking collectives, on_device(): lax.all_to_all(jnp.broadcast_to(part, (second, 1, 128)), STAGE[1], 0, 0)  22.6 us
    ppermute x8, waiting for transfers between devices, neighbour(): return lax.ppermute(x, AXES, pairs)  4.71 us
    unnamed x8, local copies, waits for them, and re-layouts  2.8 us
  transfers between devices with their start and end apart: 8, of which 2 were waited for; matrix products, arithmetic and copies ran while one was open for 0% of the time, Pallas kernels for 0%

profile of v1, /device:TPU:1, one launch (start us, length us, event | category | flops | bytes accessed | tf_op | source)
XLA Modules:
  0.0 92.5 jit_solution(8414247185099128865)
XLA Ops:
  0.6 0.0 copy-start
  0.6 1.0 %copy-done = f32[3,8,16,256]{3,2,1,0:T(8,128)S(1)} copy-done((f32[3,8,16,256]{3,2,1,0:T(8,128)S(1)}, f32[3,8,16,256]{3,2,1,0:T(8,128)}, u32[]{:S(2)}) %copy-start) | copy-done | bytes 393240
  1.6 0.0 copy-start.2
  1.6 0.9 copy-done.2
  2.5 0.0 copy-start.1
  2.5 0.1 pack.1
  2.6 4.2 %collective-permute-start = (f32[10,16,256]{2,1,0:T(8,128)S(1)}, f32[10,16,256]{2,1,0:T(8,128)S(1)}, u32[]{:S(2)}, u32[]{:S(2)}) collective-permute-start(f32[10,16,256]{2,1,0:T(8,128)S(1)} %get-tuple-element.16.up), channel_id=1, source_target_pairs={{0,128},{1,129},{2,130},{3,131},{4,132},{5,133},{6,134},{7,135},{8... | collective-permute-start | bytes 491528 | tf_op jit(solution)/shard_map/ppermute | solution.py:217
  6.8 1.3 %collective-permute-start.1 = (f32[9,16,256]{2,1,0:T(8,128)S(1)}, f32[9,16,256]{2,1,0:T(8,128)S(1)}, u32[]{:S(2)}, u32[]{:S(2)}) collective-permute-start(f32[9,16,256]{2,1,0:T(8,128)S(1)} %get-tuple-element.18), channel_id=1, source_target_pairs={{128,0},{129,1},{130,2},{131,3},{132,4},{133,5},{134,6},{135,7},{1... | collective-permute-start | bytes 442376 | tf_op jit(solution)/shard_map/ppermute | solution.py:217
  8.1 15.5 %collective-permute-start.5 = (f32[5,8,256]{2,1,0:T(8,128)S(1)}, f32[5,8,256]{2,1,0:T(8,128)S(1)}, u32[]{:S(2)}, u32[]{:S(2)}) collective-permute-start(f32[5,8,256]{2,1,0:T(8,128)S(1)} %get-tuple-element.21), channel_id=1, source_target_pairs={{1,128},{2,129},{3,130},{4,131},{5,132},{6,133},{7,134},{8,135},{9... | collective-permute-start | bytes 122888 | tf_op jit(solution)/shard_map/ppermute | solution.py:217
  23.6 1.3 %collective-permute-start.7 = (f32[4,8,256]{2,1,0:T(8,128)S(1)}, f32[4,8,256]{2,1,0:T(8,128)S(1)}, u32[]{:S(2)}, u32[]{:S(2)}) collective-permute-start(f32[4,8,256]{2,1,0:T(8,128)S(1)} %get-tuple-element.23), channel_id=1, source_target_pairs={{129,0},{130,1},{131,2},{132,3},{133,4},{134,5},{135,6},{136,7},{1... | collective-permute-start | bytes 98312 | tf_op jit(solution)/shard_map/ppermute | solution.py:217
  24.9 1.3 %collective-permute-start.6 = (f32[5,8,256]{2,1,0:T(8,128)S(1)}, f32[5,8,256]{2,1,0:T(8,128)S(1)}, u32[]{:S(2)}, u32[]{:S(2)}) collective-permute-start(f32[5,8,256]{2,1,0:T(8,128)S(1)} %get-tuple-element.22), channel_id=1, source_target_pairs={{128,1},{129,2},{130,3},{131,4},{132,5},{133,6},{134,7},{135,8},{1... | collective-permute-start | bytes 122888 | tf_op jit(solution)/shard_map/ppermute | solution.py:217
  26.2 3.5 %collective-permute-done.7.r_ne = f32[4,8,256]{2,1,0:T(8,128)S(1)} collective-permute-done((f32[4,8,256]{2,1,0:T(8,128)S(1)}, f32[4,8,256]{2,1,0:T(8,128)S(1)}, u32[]{:S(2)}, u32[]{:S(2)}) %collective-permute-start.7) | collective-permute-done | bytes 32800 | tf_op jit(solution)/shard_map/ppermute | solution.py:217
  29.7 1.9 %collective-permute-start.2 = (f32[10,8,256]{2,1,0:T(8,128)S(1)}, f32[10,8,256]{2,1,0:T(8,128)S(1)}, u32[]{:S(2)}, u32[]{:S(2)}) collective-permute-start(f32[10,8,256]{2,1,0:T(8,128)S(1)} %get-tuple-element.17.right), channel_id=1, source_target_pairs={{0,1},{1,2},{2,3},{3,4},{4,5},{5,6},{6,7},{7,8},{8,9},{9,10},{10,1... | collective-permute-start | bytes 245768 | tf_op jit(solution)/shard_map/ppermute | solution.py:217
  31.6 0.0 collective-permute-done.5.r_se
  31.6 2.4 %collective-permute-start.3 = (f32[9,8,256]{2,1,0:T(8,128)S(1)}, f32[9,8,256]{2,1,0:T(8,128)S(1)}, u32[]{:S(2)}, u32[]{:S(2)}) collective-permute-start(f32[9,8,256]{2,1,0:T(8,128)S(1)} %get-tuple-element.19), channel_id=1, source_target_pairs={{1,0},{2,1},{3,2},{4,3},{5,4},{6,5},{7,6},{8,7},{9,8},{10,9},{11,1... | collective-permute-start | bytes 221192 | tf_op jit(solution)/shard_map/ppermute | solution.py:217
  34.0 0.0 collective-permute-done.6.r_nw
  34.1 3.5 %collective-permute-start.4 = (f32[6,8,256]{2,1,0:T(8,128)S(1)}, f32[6,8,256]{2,1,0:T(8,128)S(1)}, u32[]{:S(2)}, u32[]{:S(2)}) collective-permute-start(f32[6,8,256]{2,1,0:T(8,128)S(1)} %get-tuple-element.20), channel_id=1, source_target_pairs={{0,129},{1,130},{2,131},{3,132},{4,133},{5,134},{6,135},{7,136},{8... | collective-permute-start | bytes 147464 | tf_op jit(solution)/shard_map/ppermute | solution.py:217
  37.6 1.2 %collective-permute-done.4.r_sw = f32[6,8,256]{2,1,0:T(8,128)S(1)} collective-permute-done((f32[6,8,256]{2,1,0:T(8,128)S(1)}, f32[6,8,256]{2,1,0:T(8,128)S(1)}, u32[]{:S(2)}, u32[]{:S(2)}) %collective-permute-start.4) | collective-permute-done | bytes 49184 | tf_op jit(solution)/shard_map/ppermute | solution.py:217
  38.7 0.0 collective-permute-done.3.r_r
  38.7 0.0 collective-permute-done.2.r_l
  38.8 0.0 collective-permute-done.1.r_n
  38.8 0.0 collective-permute-done.r_s
  38.8 0.0 copy-start.3
  38.8 0.9 copy-done.3
  39.7 1.0 %krylov.1 = (f32[4,16,24,256]{3,2,1,0:T(8,128)S(1)}, f32[32,1,128]{2,1,0:T(1,128)S(1)}) custom-call(f32[8,16,256]{2,1,0:T(8,128)S(1)} %get-tuple-element.14.t_own, f32[8,16,256]{2,1,0:T(8,128)S(1)} %get-tuple-element.15.d_own, f32[8,16,256]{2,1,0:T(8,128)S(1)} %copy-done.3, f32[10,16,256]{2,1,0:T(8,128)S(1)} %get-tuple-element.16.up, ...), custom_call_target="tpu_custom_call" | custom-call | tf_op jit(solution)/shard_map/krylov/pallas_call | solution.py:257
  40.7 28.1 %all_to_all.10 = f32[32,1,128]{2,1,0:T(1,128)S(1)} all-to-all(f32[32,1,128]{2,1,0:T(1,128)S(1)} %get-tuple-element.24), channel_id=1, replica_groups=mesh['y'=8,'xh'=2,'xl'=4,'z'=8,'c'=2] {'xh','z','c'}, dimensions={0} | all-to-all | bytes 32768 | tf_op jit(solution)/shard_map/all_to_all | solution.py:221
  68.8 0.1 reduce_sum.9
  68.8 22.6 %all_to_all.11.parts = f32[32,1,128]{2,1,0:T(1,128)S(1)} all-to-all(f32[32,1,128]{2,1,0:T(1,128)S(1)} %broadcast_in_dim.2), channel_id=1, replica_groups=mesh['y'=8,'xh'=2,'xl'=4,'z'=8,'c'=2] {'y','xl'}, dimensions={0} | all-to-all | bytes 32768 | tf_op jit(solution)/shard_map/all_to_all | solution.py:268
  91.5 0.0 copy-done.1
  91.5 1.1 %finish.1 = (f32[3,8,16,256]{3,2,1,0:T(8,128)}, f32[8,16,256]{2,1,0:T(8,128)}) custom-call(f32[32,1,128]{2,1,0:T(1,128)S(1)} %all_to_all.11.parts, f32[4,16,24,256]{3,2,1,0:T(8,128)S(1)} %get-tuple-element.25.v, f32[3,8,16,256]{3,2,1,0:T(8,128)S(1)} %copy-done.1), custom_call_target="tpu_custom_call" | custom-call | tf_op jit(solution)/shard_map/finish/pallas_call | solution.py:270
  (1 shorter events, 0.0 us)
Async XLA Ops:
  0.6 1.0 %copy-start = (f32[3,8,16,256]{3,2,1,0:T(8,128)S(1)}, f32[3,8,16,256]{3,2,1,0:T(8,128)}, u32[]{:S(2)}) copy-start(f32[3,8,16,256]{3,2,1,0:T(8,128)} %cot.3) | copy-start | bytes 1179652
  1.6 0.9 copy-start.2
  2.5 88.9 %copy-start.1 = (f32[3,8,16,256]{3,2,1,0:T(8,128)S(1)}, f32[3,8,16,256]{3,2,1,0:T(8,128)}, u32[]{:S(2)}) copy-start(f32[3,8,16,256]{3,2,1,0:T(8,128)} %cot.3) | copy-start | bytes 1179652
  2.6 36.1 %collective-permute-start = (f32[10,16,256]{2,1,0:T(8,128)S(1)}, f32[10,16,256]{2,1,0:T(8,128)S(1)}, u32[]{:S(2)}, u32[]{:S(2)}) collective-permute-start(f32[10,16,256]{2,1,0:T(8,128)S(1)} %get-tuple-element.16.up), channel_id=1, source_target_pairs={{0,128},{1,129},{2,130},{3,131},{4,132},{5,133},{6,134},{7,135},{8... | collective-permute-start | bytes 491528 | tf_op jit(solution)/shard_map/ppermute | solution.py:217
  6.8 31.9 %collective-permute-start.1 = (f32[9,16,256]{2,1,0:T(8,128)S(1)}, f32[9,16,256]{2,1,0:T(8,128)S(1)}, u32[]{:S(2)}, u32[]{:S(2)}) collective-permute-start(f32[9,16,256]{2,1,0:T(8,128)S(1)} %get-tuple-element.18), channel_id=1, source_target_pairs={{128,0},{129,1},{130,2},{131,3},{132,4},{133,5},{134,6},{135,7},{1... | collective-permute-start | bytes 442376 | tf_op jit(solution)/shard_map/ppermute | solution.py:217
  8.1 23.5 %collective-permute-start.5 = (f32[5,8,256]{2,1,0:T(8,128)S(1)}, f32[5,8,256]{2,1,0:T(8,128)S(1)}, u32[]{:S(2)}, u32[]{:S(2)}) collective-permute-start(f32[5,8,256]{2,1,0:T(8,128)S(1)} %get-tuple-element.21), channel_id=1, source_target_pairs={{1,128},{2,129},{3,130},{4,131},{5,132},{6,133},{7,134},{8,135},{9... | collective-permute-start | bytes 122888 | tf_op jit(solution)/shard_map/ppermute | solution.py:217
  23.6 6.1 %collective-permute-start.7 = (f32[4,8,256]{2,1,0:T(8,128)S(1)}, f32[4,8,256]{2,1,0:T(8,128)S(1)}, u32[]{:S(2)}, u32[]{:S(2)}) collective-permute-start(f32[4,8,256]{2,1,0:T(8,128)S(1)} %get-tuple-element.23), channel_id=1, source_target_pairs={{129,0},{130,1},{131,2},{132,3},{133,4},{134,5},{135,6},{136,7},{1... | collective-permute-start | bytes 98312 | tf_op jit(solution)/shard_map/ppermute | solution.py:217
  24.9 9.2 %collective-permute-start.6 = (f32[5,8,256]{2,1,0:T(8,128)S(1)}, f32[5,8,256]{2,1,0:T(8,128)S(1)}, u32[]{:S(2)}, u32[]{:S(2)}) collective-permute-start(f32[5,8,256]{2,1,0:T(8,128)S(1)} %get-tuple-element.22), channel_id=1, source_target_pairs={{128,1},{129,2},{130,3},{131,4},{132,5},{133,6},{134,7},{135,8},{1... | collective-permute-start | bytes 122888 | tf_op jit(solution)/shard_map/ppermute | solution.py:217
  29.7 9.0 %collective-permute-start.2 = (f32[10,8,256]{2,1,0:T(8,128)S(1)}, f32[10,8,256]{2,1,0:T(8,128)S(1)}, u32[]{:S(2)}, u32[]{:S(2)}) collective-permute-start(f32[10,8,256]{2,1,0:T(8,128)S(1)} %get-tuple-element.17.right), channel_id=1, source_target_pairs={{0,1},{1,2},{2,3},{3,4},{4,5},{5,6},{6,7},{7,8},{8,9},{9,10},{10,1... | collective-permute-start | bytes 245768 | tf_op jit(solution)/shard_map/ppermute | solution.py:217
  31.6 7.1 %collective-permute-start.3 = (f32[9,8,256]{2,1,0:T(8,128)S(1)}, f32[9,8,256]{2,1,0:T(8,128)S(1)}, u32[]{:S(2)}, u32[]{:S(2)}) collective-permute-start(f32[9,8,256]{2,1,0:T(8,128)S(1)} %get-tuple-element.19), channel_id=1, source_target_pairs={{1,0},{2,1},{3,2},{4,3},{5,4},{6,5},{7,6},{8,7},{9,8},{10,9},{11,1... | collective-permute-start | bytes 221192 | tf_op jit(solution)/shard_map/ppermute | solution.py:217
  34.1 4.7 %collective-permute-start.4 = (f32[6,8,256]{2,1,0:T(8,128)S(1)}, f32[6,8,256]{2,1,0:T(8,128)S(1)}, u32[]{:S(2)}, u32[]{:S(2)}) collective-permute-start(f32[6,8,256]{2,1,0:T(8,128)S(1)} %get-tuple-element.20), channel_id=1, source_target_pairs={{0,129},{1,130},{2,131},{3,132},{4,133},{5,134},{6,135},{7,136},{8... | collective-permute-start | bytes 147464 | tf_op jit(solution)/shard_map/ppermute | solution.py:217
  38.8 0.9 copy-start.3

commit v2 on v1

--- a/solution.py
+++ b/solution.py
@@ -14,7 +14,7 @@
 SPLIT = 0.6
 NMOM = 2 * ITERS
 AXES = ("y", "xh", "xl", "z", "c")
-STAGE = (("xh", "z", "c"), ("y", "xl"))
+STAGE = (("xh", "z"), ("y", "xl", "c"))
 F32 = jnp.float32
 
 
@@ -22,87 +22,81 @@
     return lax.broadcasted_iota(jnp.int32, shape, axis)
 
 
-def pack_kernel(cot, coef, t_out, d_out, up, down, right, left, up_r, up_l, down_r, down_l):
+def pack_kernel(cot_hbm, coef_hbm, t_out, d_out, scaling, up, down, cot, coef, sems):
+    copies = [
+        pltpu.make_async_copy(coef_hbm, coef, sems.at[0]),
+        pltpu.make_async_copy(cot_hbm, cot, sems.at[1]),
+    ]
+    for copy in copies:
+        copy.start()
+    for copy in copies:
+        copy.wait()
     ny, nx, nz = coef.shape
     sub, lane = iota((nx, nz), 0), iota((nx, nz), 1)
-    sub8 = iota((8, nz), 0)
-    column = jnp.zeros((8, nz), F32)
+    column = jnp.zeros((nx, nz), F32)
     for y in range(ny):
         c0, c1, c2 = cot[0, y], cot[1, y], cot[2, y]
-        d = 1.0 / (6.0 + coef[y])
+        m = 6.0 + coef[y]
+        d = 1.0 / m
         t = jnp.where(sub == 0, 0.0, pltpu.roll(c1, 1, 0)) - c1
         t = t + (jnp.where(lane == 0, 0.0, pltpu.roll(c2, 1, 1)) - c2)
         t = t + ((cot[0, y - 1] - c0) if y else -c0)
         t_out[y] = t
         d_out[y] = d
-        to_right = jnp.where(sub8 >= 4, t[nx - 8 :], pltpu.roll(d[nx - 8 :], 4, 0))
-        to_left = jnp.where(sub8 < 4, t[:8], pltpu.roll(d[:8], 4, 0))
-        right[y] = to_right
-        left[y] = to_left
+        scaling[y] = m
         if y < HALO:
             down[y], down[HALO + y] = t, d
-            down_r[y], down_l[y] = to_right, to_left
         if y >= ny - HALO:
             j = y - (ny - HALO)
             up[j], up[HALO + j] = t, d
-            up_r[j], up_l[j] = to_right, to_left
-        column = jnp.where(sub8 == y, jnp.broadcast_to(c1[nx - 1 : nx], (8, nz)), column)
-    edge = cot[0, ny - 1]
-    up[2 * HALO] = edge
-    right[ny] = edge[nx - 8 :]
-    left[ny] = edge[:8]
-    up_r[HALO] = edge[nx - 8 :]
-    up_l[HALO] = edge[:8]
-    right[ny + 1] = column
-    up_r[HALO + 1] = column
-    down_r[HALO] = column
-    wide = jnp.concatenate([column, jnp.zeros((nx - 8, nz), F32)], axis=0)
-    up[2 * HALO + 1] = wide
-    down[2 * HALO] = wide
-
-
-def krylov_kernel(t_own, d_own, coef, up, right, r_s, r_n, r_l, r_r, r_sw, r_se, r_nw, r_ne, v, part, dw):
-    ny, nx, nz = coef.shape
+        column = jnp.where(sub == y, jnp.broadcast_to(c1[nx - 1 : nx], (nx, nz)), column)
+    up[2 * HALO] = cot[0, ny - 1]
+    up[2 * HALO + 1] = column
+    down[2 * HALO] = column
+
+
+def window_rows(t_own, d_own, up, r_s, r_n):
+    ny = t_own.shape[0]
+    out = []
+    for y in range(ny):
+        t = t_own[y]
+        out.append((t + r_s[2 * HALO] if y == 0 else t, d_own[y]))
+    for j in range(HALO):
+        t = r_n[j]
+        out.append((t + up[2 * HALO] if j == 0 else t, r_n[HALO + j]))
+    return out + [(r_s[j], r_s[HALO + j]) for j in range(HALO)]
+
+
+def side_kernel(t_own, d_own, up, r_s, r_n, right, left):
+    ny, nx, nz = t_own.shape
+    low = iota((8, nz), 0) < 4
+    for row, (t, d) in enumerate(window_rows(t_own, d_own, up, r_s, r_n)):
+        right[row] = jnp.where(low, pltpu.roll(d[nx - 8 :], 4, 0), t[nx - 8 :])
+        left[row] = jnp.where(low, t[:8], pltpu.roll(d[:8], 4, 0))
+    rows = ny + 2 * HALO
+    right[rows] = up[2 * HALO + 1, :8]
+    right[rows + 1] = jnp.where(low, r_n[2 * HALO, :8], r_s[2 * HALO + 1, :8])
+
+
+def krylov_kernel(t_own, d_own, scaling_own, up, right, r_s, r_n, r_l, r_r, v, part, dw):
+    ny, nx, nz = t_own.shape
     sub8 = iota((8, nz), 0)
     lane = iota((nx + 8, nz), 1)
     low = sub8 < 4
-
-    def at_first(col_ref_value, k):
-        return jnp.where(sub8 == 0, jnp.broadcast_to(col_ref_value[k : k + 1], (8, nz)), 0.0)
-
-    def assemble(row, t, d, from_left, from_right, edge, edge_side, col_low, col_high, k):
-        t_side = jnp.where(low, from_right, from_left)
-        d_side = pltpu.roll(jnp.where(low, from_left, from_right), 4, 0)
-        if edge is not None:
-            t = t + edge
-            t_side = t_side + edge_side
-        t_first = t[:8] + at_first(col_low, k)
-        t_side = t_side + at_first(col_high, k)
-        v[0, row, 0:8] = t_first * d[:8]
+    columns = [(r_l[ny + 2 * HALO + i], right[ny + 2 * HALO + i]) for i in range(2)]
+
+    def at_first(column, k):
+        return jnp.where(sub8 == 0, jnp.broadcast_to(column[k : k + 1], (8, nz)), 0.0)
+
+    for row, (t, d) in enumerate(window_rows(t_own, d_own, up, r_s, r_n)):
+        before, after = columns[row // 8]
+        v[0, row, 0:8] = (t[:8] + at_first(before, row % 8)) * d[:8]
         v[0, row, 8:nx] = t[8:] * d[8:]
-        v[0, row, nx : nx + 8] = t_side * d_side
+        t = jnp.where(low, r_r[row], r_l[row]) + at_first(after, row % 8)
+        d_side = pltpu.roll(jnp.where(low, r_l[row], r_r[row]), 4, 0)
+        v[0, row, nx : nx + 8] = t * d_side
         dw[row, 0:nx] = d
         dw[row, nx : nx + 8] = d_side
-
-    own_low, own_high = r_l[ny + 1], right[ny + 1]
-    for y in range(ny):
-        edge = edge_side = None
-        if y == 0:
-            edge = r_s[2 * HALO]
-            edge_side = jnp.where(low, r_se[HALO], r_sw[HALO])
-        assemble(y, t_own[y], d_own[y], r_l[y], r_r[y], edge, edge_side, own_low, own_high, y)
-    col_low, col_high = r_nw[HALO], r_n[2 * HALO][:8]
-    for j in range(HALO):
-        edge = edge_side = None
-        if j == 0:
-            edge = up[2 * HALO]
-            edge_side = jnp.where(low, r_r[ny], r_l[ny])
-        assemble(ny + j, r_n[j], r_n[HALO + j], r_nw[j], r_ne[j], edge, edge_side, col_low, col_high, j)
-    col_low, col_high = r_sw[HALO + 1], r_s[2 * HALO + 1][:8]
-    for j in range(HALO):
-        assemble(
-            ny + HALO + j, r_s[j], r_s[HALO + j], r_sw[j], r_se[j], None, None, col_low, col_high, ny - HALO + j
-        )
 
     rows = ny + 2 * HALO
 
@@ -121,7 +115,7 @@
             v[k + 1, row % rows] = powered(k, row)
     total = [jnp.zeros((8, 128), F32) for _ in range(NMOM * len(SHIFTS))]
     for y in range(ny):
-        scaling = 6.0 + coef[y]
+        scaling = scaling_own[y]
         last = powered(ITERS - 1, y)
         for a in range(0, nx, 8):
             for b in range(0, nz, 128):
@@ -223,37 +217,37 @@
 
 def on_device(gy, gx, sizes, cotangent, coefficient):
     ny, nx, nz = coefficient.shape
+    limit = pltpu.CompilerParams(vmem_limit_bytes=24 * 1024 * 1024)
+    send = functools.partial(neighbour, ny=gy, nx=gx)
+
+    def shapes(*sizes):
+        return [jax.ShapeDtypeStruct(s, F32) for s in sizes]
+
+    rows, wide = ny + 2 * HALO, nx + 8
     block = (ny, nx, nz)
-    shapes = [
-        block,
-        block,
-        (2 * HALO + 2, nx, nz),
-        (2 * HALO + 1, nx, nz),
-        (ny + 2, 8, nz),
-        (ny + 1, 8, nz),
-        (HALO + 2, 8, nz),
-        (HALO + 1, 8, nz),
-        (HALO + 1, 8, nz),
-        (HALO, 8, nz),
-    ]
-    limit = pltpu.CompilerParams(vmem_limit_bytes=24 * 1024 * 1024)
-    t, d, up, down, right, left, up_r, up_l, down_r, down_l = pl.pallas_call(
+    t, d, scaling, up, down = pl.pallas_call(
         pack_kernel,
-        out_shape=[jax.ShapeDtypeStruct(s, F32) for s in shapes],
+        in_specs=[pl.BlockSpec(memory_space=pltpu.HBM)] * 2,
+        out_shape=shapes(block, block, block, (2 * HALO + 2, nx, nz), (2 * HALO + 1, nx, nz)),
+        scratch_shapes=[
+            pltpu.VMEM(cotangent.shape, F32),
+            pltpu.VMEM(block, F32),
+            pltpu.SemaphoreType.DMA((2,)),
+        ],
         compiler_params=limit,
         name="pack",
     )(cotangent, coefficient)
-    send = functools.partial(neighbour, ny=gy, nx=gx)
-    r_sw = send(up_r, 1, 1)
-    r_se = send(up_l, 1, -1)
-    r_nw = send(down_r, -1, 1)
-    r_ne = send(down_l, -1, -1)
     r_s = send(up, 1, 0)
     r_n = send(down, -1, 0)
+    right, left = pl.pallas_call(
+        side_kernel,
+        out_shape=shapes((rows + 2, 8, nz), (rows, 8, nz)),
+        compiler_params=limit,
+        name="side",
+    )(t, d, up, r_s, r_n)
     r_l = send(right, 0, 1)
     r_r = send(left, 0, -1)
     first, second = (int(np.prod([sizes[a] for a in axes])) for axes in STAGE)
-    rows, wide = ny + 2 * HALO, nx + 8
     v, part = pl.pallas_call(
         krylov_kernel,
         out_shape=[
@@ -263,7 +257,7 @@
         scratch_shapes=[pltpu.VMEM((rows, wide, nz), F32)],
         compiler_params=limit,
         name="krylov",
-    )(t, d, coefficient, up, right, r_s, r_n, r_l, r_r, r_sw, r_se, r_nw, r_ne)
+    )(t, d, scaling, up, right, r_s, r_n, r_l, r_r)
     part = exchange_sum(part, STAGE[0])
     part = lax.all_to_all(jnp.broadcast_to(part, (second, 1, 128)), STAGE[1], 0, 0)
     return tuple(
@@ -281,7 +275,7 @@
 
 def solution(mesh):
     gy, gx = mesh.shape["gy"], mesh.shape["gx"]
-    fine = Mesh(np.asarray(mesh.devices).reshape(gy, 2, gx // 32, 8, 2), AXES)
+    fine = Mesh(np.asarray(mesh.devices).reshape(gy, gx // 32, 2, 8, 2), AXES)
     along_x = AXES[1:]
     wide, flat = P(None, AXES[0], along_x, None), P(AXES[0], along_x, None)
     return jax.shard_map(

time: 93 us -> 75.3 us (0.81)
  starting transfers between devices: 31.3 us -> 21.1 us
  blocking collectives: 50.7 us -> 43.1 us
    ppermute x8 -> x4, starting transfers between devices: 31.3 us -> 21.1 us  [neighbour(): return lax.ppermute(x, AXES, pairs)]
    all_to_all x1, blocking collectives: 22.6 us -> 15.7 us  [on_device(): lax.all_to_all(jnp.broadcast_to(part, (second, 1, 128)), STAGE[1], 0, 0)]
    unnamed x8 -> x6, local copies, waits for them, and re-layouts: 2.8 us -> 1.9 us
    ppermute x8 -> x4, waiting for transfers between devices: 4.71 us -> 5.56 us  [neighbour(): return lax.ppermute(x, AXES, pairs)]
  transfers between devices with their start and end apart: 8 -> 4, of which waited for: 2 -> 2; matrix products, arithmetic and copies ran while one was open for 0% -> 0% of each run, Pallas kernels for 0% -> 0%
where the time goes in v2:
time: 75.3 us; the launch traced here: 75 us
  blocking collectives  43.1 us (57%)
  starting transfers between devices  21.1 us (28%)
  waiting for transfers between devices  5.56 us (7%)
  Pallas kernels  2.58 us (3%)
  local copies, waits for them, and re-layouts  1.91 us (3%)
    all_to_all x1, blocking collectives, exchange_sum(): return jnp.sum(lax.all_to_all(x, axes, 0, 0), axis=0, keepdims=True)  27.5 us
    ppermute x4, starting transfers between devices, neighbour(): return lax.ppermute(x, AXES, pairs)  21.1 us
    all_to_all x1, blocking collectives, on_device(): lax.all_to_all(jnp.broadcast_to(part, (second, 1, 128)), STAGE[1], 0, 0)  15.7 us
    ppermute x4, waiting for transfers between devices, neighbour(): return lax.ppermute(x, AXES, pairs)  5.56 us
    unnamed x6, local copies, waits for them, and re-layouts  1.9 us
  transfers between devices with their start and end apart: 4, of which 2 were waited for; matrix products, arithmetic and copies ran while one was open for 0% of the time, Pallas kernels for 0%

profile of v2, /device:TPU:1, one launch (start us, length us, event | category | flops | bytes accessed | tf_op | source)
XLA Modules:
  0.0 75.0 jit_solution(16813877467207072462)
XLA Ops:
  0.6 0.0 copy-start
  0.6 1.0 %copy-done = f32[3,8,16,256]{3,2,1,0:T(8,128)S(1)} copy-done((f32[3,8,16,256]{3,2,1,0:T(8,128)S(1)}, f32[3,8,16,256]{3,2,1,0:T(8,128)}, u32[]{:S(2)}) %copy-start) | copy-done | bytes 393240
  1.6 0.0 copy-start.2
  1.6 0.9 %copy-done.2 = f32[8,16,256]{2,1,0:T(8,128)S(1)} copy-done((f32[8,16,256]{2,1,0:T(8,128)S(1)}, f32[8,16,256]{2,1,0:T(8,128)}, u32[]{:S(2)}) %copy-start.2) | copy-done | bytes 131096
  2.5 0.0 copy-start.1
  2.5 0.5 pack.1
  3.0 4.2 %collective-permute-start = (f32[10,16,256]{2,1,0:T(8,128)S(1)}, f32[10,16,256]{2,1,0:T(8,128)S(1)}, u32[]{:S(2)}, u32[]{:S(2)}) collective-permute-start(f32[10,16,256]{2,1,0:T(8,128)S(1)} %get-tuple-element.14.up), channel_id=1, source_target_pairs={{0,128},{1,129},{2,130},{3,131},{4,132},{5,133},{6,134},{7,135},{8... | collective-permute-start | bytes 491528 | tf_op jit(solution)/shard_map/ppermute | solution.py:211
  7.2 1.3 %collective-permute-start.1 = (f32[9,16,256]{2,1,0:T(8,128)S(1)}, f32[9,16,256]{2,1,0:T(8,128)S(1)}, u32[]{:S(2)}, u32[]{:S(2)}) collective-permute-start(f32[9,16,256]{2,1,0:T(8,128)S(1)} %get-tuple-element.15), channel_id=1, source_target_pairs={{128,0},{129,1},{130,2},{131,3},{132,4},{133,5},{134,6},{135,7},{1... | collective-permute-start | bytes 442376 | tf_op jit(solution)/shard_map/ppermute | solution.py:211
  8.5 4.6 %collective-permute-done.1.r_n = f32[9,16,256]{2,1,0:T(8,128)S(1)} collective-permute-done((f32[9,16,256]{2,1,0:T(8,128)S(1)}, f32[9,16,256]{2,1,0:T(8,128)S(1)}, u32[]{:S(2)}, u32[]{:S(2)}) %collective-permute-start.1) | collective-permute-done | bytes 147488 | tf_op jit(solution)/shard_map/ppermute | solution.py:211
  13.1 0.0 collective-permute-done.r_s
  13.1 7.1 %collective-permute-start.2 = (f32[18,8,256]{2,1,0:T(8,128)S(1)}, f32[18,8,256]{2,1,0:T(8,128)S(1)}, u32[]{:S(2)}, u32[]{:S(2)}) collective-permute-start(f32[18,8,256]{2,1,0:T(8,128)S(1)} %get-tuple-element.16.right), channel_id=1, source_target_pairs={{0,1},{1,2},{2,3},{3,4},{4,5},{5,6},{6,7},{7,8},{8,9},{9,10},{10,1... | collective-permute-start | bytes 442376 | tf_op jit(solution)/shard_map/ppermute | solution.py:211
  20.2 8.6 %collective-permute-start.3 = (f32[16,8,256]{2,1,0:T(8,128)S(1)}, f32[16,8,256]{2,1,0:T(8,128)S(1)}, u32[]{:S(2)}, u32[]{:S(2)}) collective-permute-start(f32[16,8,256]{2,1,0:T(8,128)S(1)} %get-tuple-element.17), channel_id=1, source_target_pairs={{1,0},{2,1},{3,2},{4,3},{5,4},{6,5},{7,6},{8,7},{9,8},{10,9},{11,1... | collective-permute-start | bytes 393224 | tf_op jit(solution)/shard_map/ppermute | solution.py:211
  28.8 1.0 %collective-permute-done.3.r_r = f32[16,8,256]{2,1,0:T(8,128)S(1)} collective-permute-done((f32[16,8,256]{2,1,0:T(8,128)S(1)}, f32[16,8,256]{2,1,0:T(8,128)S(1)}, u32[]{:S(2)}, u32[]{:S(2)}) %collective-permute-start.3) | collective-permute-done | bytes 131104 | tf_op jit(solution)/shard_map/ppermute | solution.py:211
  29.7 0.0 collective-permute-done.2.r_l
  29.7 1.0 %krylov.1 = (f32[4,16,24,256]{3,2,1,0:T(8,128)S(1)}, f32[32,1,128]{2,1,0:T(1,128)S(1)}) custom-call(f32[8,16,256]{2,1,0:T(8,128)S(1)} %get-tuple-element.11.t_own, f32[8,16,256]{2,1,0:T(8,128)S(1)} %get-tuple-element.12.d_own, f32[8,16,256]{2,1,0:T(8,128)S(1)} %get-tuple-element.13.scaling_own, f32[10,16,256]{2,1,0:T(8,128)S(1)} %get-tuple-element.14.up, ...), custom_call_target="tpu_custom_call" | custom-call | tf_op jit(solution)/shard_map/krylov/pallas_call | solution.py:251
  30.7 27.5 %all_to_all.10 = f32[32,1,128]{2,1,0:T(1,128)S(1)} all-to-all(f32[32,1,128]{2,1,0:T(1,128)S(1)} %get-tuple-element.18), channel_id=1, replica_groups=mesh['y'=8,'xh'=4,'xl'=2,'z'=8,'c'=2] {'xh','z'}, dimensions={0} | all-to-all | bytes 32768 | tf_op jit(solution)/shard_map/all_to_all | solution.py:215
  58.2 0.1 reduce_sum.9
  58.3 15.7 %all_to_all.11.parts = f32[32,1,128]{2,1,0:T(1,128)S(1)} all-to-all(f32[32,1,128]{2,1,0:T(1,128)S(1)} %broadcast_in_dim.2), channel_id=1, replica_groups=mesh['y'=8,'xh'=4,'xl'=2,'z'=8,'c'=2] {'y','xl','c'}, dimensions={0} | all-to-all | bytes 32768 | tf_op jit(solution)/shard_map/all_to_all | solution.py:262
  73.9 0.0 copy-done.1
  73.9 1.1 %finish.1 = (f32[3,8,16,256]{3,2,1,0:T(8,128)}, f32[8,16,256]{2,1,0:T(8,128)}) custom-call(f32[32,1,128]{2,1,0:T(1,128)S(1)} %all_to_all.11.parts, f32[4,16,24,256]{3,2,1,0:T(8,128)S(1)} %get-tuple-element.19.v, f32[3,8,16,256]{3,2,1,0:T(8,128)S(1)} %copy-done.1), custom_call_target="tpu_custom_call" | custom-call | tf_op jit(solution)/shard_map/finish/pallas_call | solution.py:264
  (2 shorter events, 0.0 us)
Async XLA Ops:
  0.6 1.0 %copy-start = (f32[3,8,16,256]{3,2,1,0:T(8,128)S(1)}, f32[3,8,16,256]{3,2,1,0:T(8,128)}, u32[]{:S(2)}) copy-start(f32[3,8,16,256]{3,2,1,0:T(8,128)} %cot.1) | copy-start | bytes 1179652
  1.6 0.9 %copy-start.2 = (f32[8,16,256]{2,1,0:T(8,128)S(1)}, f32[8,16,256]{2,1,0:T(8,128)}, u32[]{:S(2)}) copy-start(f32[8,16,256]{2,1,0:T(8,128)} %coef_hbm.1) | copy-start | bytes 393220
  2.5 71.4 %copy-start.1 = (f32[3,8,16,256]{3,2,1,0:T(8,128)S(1)}, f32[3,8,16,256]{3,2,1,0:T(8,128)}, u32[]{:S(2)}) copy-start(f32[3,8,16,256]{3,2,1,0:T(8,128)} %cot.1) | copy-start | bytes 1179652
  3.0 10.1 %collective-permute-start = (f32[10,16,256]{2,1,0:T(8,128)S(1)}, f32[10,16,256]{2,1,0:T(8,128)S(1)}, u32[]{:S(2)}, u32[]{:S(2)}) collective-permute-start(f32[10,16,256]{2,1,0:T(8,128)S(1)} %get-tuple-element.14.up), channel_id=1, source_target_pairs={{0,128},{1,129},{2,130},{3,131},{4,132},{5,133},{6,134},{7,135},{8... | collective-permute-start | bytes 491528 | tf_op jit(solution)/shard_map/ppermute | solution.py:211
  7.2 5.9 %collective-permute-start.1 = (f32[9,16,256]{2,1,0:T(8,128)S(1)}, f32[9,16,256]{2,1,0:T(8,128)S(1)}, u32[]{:S(2)}, u32[]{:S(2)}) collective-permute-start(f32[9,16,256]{2,1,0:T(8,128)S(1)} %get-tuple-element.15), channel_id=1, source_target_pairs={{128,0},{129,1},{130,2},{131,3},{132,4},{133,5},{134,6},{135,7},{1... | collective-permute-start | bytes 442376 | tf_op jit(solution)/shard_map/ppermute | solution.py:211
  13.1 16.6 %collective-permute-start.2 = (f32[18,8,256]{2,1,0:T(8,128)S(1)}, f32[18,8,256]{2,1,0:T(8,128)S(1)}, u32[]{:S(2)}, u32[]{:S(2)}) collective-permute-start(f32[18,8,256]{2,1,0:T(8,128)S(1)} %get-tuple-element.16.right), channel_id=1, source_target_pairs={{0,1},{1,2},{2,3},{3,4},{4,5},{5,6},{6,7},{7,8},{8,9},{9,10},{10,1... | collective-permute-start | bytes 442376 | tf_op jit(solution)/shard_map/ppermute | solution.py:211
  20.2 9.6 %collective-permute-start.3 = (f32[16,8,256]{2,1,0:T(8,128)S(1)}, f32[16,8,256]{2,1,0:T(8,128)S(1)}, u32[]{:S(2)}, u32[]{:S(2)}) collective-permute-start(f32[16,8,256]{2,1,0:T(8,128)S(1)} %get-tuple-element.17), channel_id=1, source_target_pairs={{1,0},{2,1},{3,2},{4,3},{5,4},{6,5},{7,6},{8,7},{9,8},{10,9},{11,1... | collective-permute-start | bytes 393224 | tf_op jit(solution)/shard_map/ppermute | solution.py:211

commit v3 on v2

--- a/solution.py
+++ b/solution.py
@@ -67,23 +67,35 @@
     return out + [(r_s[j], r_s[HALO + j]) for j in range(HALO)]
 
 
-def side_kernel(t_own, d_own, up, r_s, r_n, right, left):
+def side_kernel(odd, t_own, d_own, up, r_s, r_n, to_core, to_chip):
     ny, nx, nz = t_own.shape
     low = iota((8, nz), 0) < 4
+    even = odd[0] == 0
     for row, (t, d) in enumerate(window_rows(t_own, d_own, up, r_s, r_n)):
-        right[row] = jnp.where(low, pltpu.roll(d[nx - 8 :], 4, 0), t[nx - 8 :])
-        left[row] = jnp.where(low, t[:8], pltpu.roll(d[:8], 4, 0))
+        right = jnp.where(low, pltpu.roll(d[nx - 8 :], 4, 0), t[nx - 8 :])
+        left = jnp.where(low, t[:8], pltpu.roll(d[:8], 4, 0))
+        to_core[row] = jnp.where(even, right, left)
+        to_chip[row] = jnp.where(even, left, right)
     rows = ny + 2 * HALO
-    right[rows] = up[2 * HALO + 1, :8]
-    right[rows + 1] = jnp.where(low, r_n[2 * HALO, :8], r_s[2 * HALO + 1, :8])
-
-
-def krylov_kernel(t_own, d_own, scaling_own, up, right, r_s, r_n, r_l, r_r, v, part, dw):
+    for to in (to_core, to_chip):
+        to[rows] = up[2 * HALO + 1, :8]
+        to[rows + 1] = jnp.where(low, r_n[2 * HALO, :8], r_s[2 * HALO + 1, :8])
+
+
+def krylov_kernel(odd, t_own, d_own, scaling_own, up, to_core, r_s, r_n, r_core, r_chip, v, part, dw):
     ny, nx, nz = t_own.shape
     sub8 = iota((8, nz), 0)
     lane = iota((nx + 8, nz), 1)
     low = sub8 < 4
-    columns = [(r_l[ny + 2 * HALO + i], right[ny + 2 * HALO + i]) for i in range(2)]
+    even = odd[0] == 0
+
+    def from_left(row):
+        return jnp.where(even, r_chip[row], r_core[row])
+
+    def from_right(row):
+        return jnp.where(even, r_core[row], r_chip[row])
+
+    columns = [(from_left(ny + 2 * HALO + i), to_core[ny + 2 * HALO + i]) for i in range(2)]
 
     def at_first(column, k):
         return jnp.where(sub8 == 0, jnp.broadcast_to(column[k : k + 1], (8, nz)), 0.0)
@@ -92,8 +104,9 @@
         before, after = columns[row // 8]
         v[0, row, 0:8] = (t[:8] + at_first(before, row % 8)) * d[:8]
         v[0, row, 8:nx] = t[8:] * d[8:]
-        t = jnp.where(low, r_r[row], r_l[row]) + at_first(after, row % 8)
-        d_side = pltpu.roll(jnp.where(low, r_l[row], r_r[row]), 4, 0)
+        left, right = from_left(row), from_right(row)
+        t = jnp.where(low, right, left) + at_first(after, row % 8)
+        d_side = pltpu.roll(jnp.where(low, left, right), 4, 0)
         v[0, row, nx : nx + 8] = t * d_side
         dw[row, 0:nx] = d
         dw[row, nx : nx + 8] = d_side
@@ -201,14 +214,13 @@
         here = above
 
 
-def neighbour(x, dy, dx, ny, nx):
-    pairs = [
-        (a * nx + b, (a + dy) * nx + b + dx)
-        for a in range(ny)
-        for b in range(nx)
-        if 0 <= a + dy < ny and 0 <= b + dx < nx
-    ]
-    return lax.ppermute(x, AXES, pairs)
+def along_y(x, dy, ny, nx):
+    return lax.ppermute(x, AXES, [(a * nx + b, (a + dy) * nx + b) for a in range(ny) for b in range(nx) if 0 <= a + dy < ny])
+
+
+def pairs_along_x(x, first, ny, nx):
+    up = [(a * nx + b, a * nx + b + 1) for a in range(ny) for b in range(first, nx - 1, 2)]
+    return lax.ppermute(x, AXES, up + [(j, i) for i, j in up])
 
 
 def exchange_sum(x, axes):
@@ -218,7 +230,6 @@
 def on_device(gy, gx, sizes, cotangent, coefficient):
     ny, nx, nz = coefficient.shape
     limit = pltpu.CompilerParams(vmem_limit_bytes=24 * 1024 * 1024)
-    send = functools.partial(neighbour, ny=gy, nx=gx)
 
     def shapes(*sizes):
         return [jax.ShapeDtypeStruct(s, F32) for s in sizes]
@@ -237,19 +248,25 @@
         compiler_params=limit,
         name="pack",
     )(cotangent, coefficient)
-    r_s = send(up, 1, 0)
-    r_n = send(down, -1, 0)
-    right, left = pl.pallas_call(
+    r_s = along_y(up, 1, gy, gx)
+    r_n = along_y(down, -1, gy, gx)
+    odd = lax.axis_index("c").astype(jnp.int32).reshape(1)
+    scalar = pl.BlockSpec(memory_space=pltpu.SMEM)
+    whole = pl.BlockSpec(memory_space=pltpu.VMEM)
+    side = (rows + 2, 8, nz)
+    to_core, to_chip = pl.pallas_call(
         side_kernel,
-        out_shape=shapes((rows + 2, 8, nz), (rows, 8, nz)),
+        in_specs=[scalar] + [whole] * 5,
+        out_shape=shapes(side, side),
         compiler_params=limit,
         name="side",
-    )(t, d, up, r_s, r_n)
-    r_l = send(right, 0, 1)
-    r_r = send(left, 0, -1)
+    )(odd, t, d, up, r_s, r_n)
+    r_chip = pairs_along_x(to_chip, 1, gy, gx)
+    r_core = pairs_along_x(to_core, 0, gy, gx)
     first, second = (int(np.prod([sizes[a] for a in axes])) for axes in STAGE)
     v, part = pl.pallas_call(
         krylov_kernel,
+        in_specs=[scalar] + [whole] * 9,
         out_shape=[
             jax.ShapeDtypeStruct((ITERS, rows, wide, nz), F32),
             jax.ShapeDtypeStruct((first, 1, 128), F32),
@@ -257,7 +274,7 @@
         scratch_shapes=[pltpu.VMEM((rows, wide, nz), F32)],
         compiler_params=limit,
         name="krylov",
-    )(t, d, scaling, up, right, r_s, r_n, r_l, r_r)
+    )(odd, t, d, scaling, up, to_core, r_s, r_n, r_core, r_chip)
     part = exchange_sum(part, STAGE[0])
     part = lax.all_to_all(jnp.broadcast_to(part, (second, 1, 128)), STAGE[1], 0, 0)
     return tuple(

time: 75.3 us -> 73.7 us (0.979)
  blocking collectives: 43.1 us -> 42.1 us
    all_to_all x1, blocking collectives: 27.5 us -> 25.5 us  [exchange_sum(): return jnp.sum(lax.all_to_all(x, axes, 0, 0), axis=0, keepdims=True)]
    all_to_all x1, blocking collectives: 15.7 us -> 16.6 us  [on_device(): lax.all_to_all(jnp.broadcast_to(part, (second, 1, 128)), STAGE[1], 0, 0)]
where the time goes in v3:
time: 73.7 us; the launch traced here: 73.4 us
  blocking collectives  42.1 us (57%)
  starting transfers between devices  20.5 us (28%)
  waiting for transfers between devices  5.56 us (8%)
  Pallas kernels  2.59 us (4%)
  local copies, waits for them, and re-layouts  1.91 us (3%)
    all_to_all x1, blocking collectives, exchange_sum(): return jnp.sum(lax.all_to_all(x, axes, 0, 0), axis=0, keepdims=True)  25.5 us
    all_to_all x1, blocking collectives, on_device(): lax.all_to_all(jnp.broadcast_to(part, (second, 1, 128)), STAGE[1], 0, 0)  16.6 us
    ppermute x2, starting transfers between devices, pairs_along_x(): return lax.ppermute(x, AXES, up + [(j, i) for i, j in up])  15 us
    ppermute x2, starting transfers between devices, along_y(): lax.ppermute(x, AXES, [(a * nx + b, (a + dy) * nx + b) for a in range(ny)...  5.45 us
    ppermute x2, waiting for transfers between devices, along_y(): lax.ppermute(x, AXES, [(a * nx + b, (a + dy) * nx + b) for a in range(ny)...  4.59 us
    unnamed x6, local copies, waits for them, and re-layouts  1.9 us
  transfers between devices with their start and end apart: 4, of which 2 were waited for; matrix products, arithmetic and copies ran while one was open for 0% of the time, Pallas kernels for 0%

profile of v3, /device:TPU:1, one launch (start us, length us, event | category | flops | bytes accessed | tf_op | source)
XLA Modules:
  0.0 73.4 jit_solution(10524068076795115961)
XLA Ops:
  0.6 0.0 copy-start
  0.6 1.0 %copy-done = f32[3,8,16,256]{3,2,1,0:T(8,128)S(1)} copy-done((f32[3,8,16,256]{3,2,1,0:T(8,128)S(1)}, f32[3,8,16,256]{3,2,1,0:T(8,128)}, u32[]{:S(2)}) %copy-start) | copy-done | bytes 393240
  1.6 0.0 copy-start.2
  1.6 0.9 %copy-done.2 = f32[8,16,256]{2,1,0:T(8,128)S(1)} copy-done((f32[8,16,256]{2,1,0:T(8,128)S(1)}, f32[8,16,256]{2,1,0:T(8,128)}, u32[]{:S(2)}) %copy-start.2) | copy-done | bytes 131096
  2.5 0.0 copy-start.1
  2.5 0.5 pack.1
  3.0 4.2 %collective-permute-start = (f32[10,16,256]{2,1,0:T(8,128)S(1)}, f32[10,16,256]{2,1,0:T(8,128)S(1)}, u32[]{:S(2)}, u32[]{:S(2)}) collective-permute-start(f32[10,16,256]{2,1,0:T(8,128)S(1)} %get-tuple-element.14.up), channel_id=1, source_target_pairs={{0,128},{1,129},{2,130},{3,131},{4,132},{5,133},{6,134},{7,135},{8... | collective-permute-start | bytes 491528 | tf_op jit(solution)/shard_map/ppermute | solution.py:218
  7.2 1.3 %collective-permute-start.1 = (f32[9,16,256]{2,1,0:T(8,128)S(1)}, f32[9,16,256]{2,1,0:T(8,128)S(1)}, u32[]{:S(2)}, u32[]{:S(2)}) collective-permute-start(f32[9,16,256]{2,1,0:T(8,128)S(1)} %get-tuple-element.15), channel_id=1, source_target_pairs={{128,0},{129,1},{130,2},{131,3},{132,4},{133,5},{134,6},{135,7},{1... | collective-permute-start | bytes 442376 | tf_op jit(solution)/shard_map/ppermute | solution.py:218
  8.5 4.6 %collective-permute-done.1.r_n = f32[9,16,256]{2,1,0:T(8,128)S(1)} collective-permute-done((f32[9,16,256]{2,1,0:T(8,128)S(1)}, f32[9,16,256]{2,1,0:T(8,128)S(1)}, u32[]{:S(2)}, u32[]{:S(2)}) %collective-permute-start.1) | collective-permute-done | bytes 147488 | tf_op jit(solution)/shard_map/ppermute | solution.py:218
  13.1 0.0 collective-permute-done.r_s
  13.1 7.1 %collective-permute-start.3 = (f32[18,8,256]{2,1,0:T(8,128)S(1)}, f32[18,8,256]{2,1,0:T(8,128)S(1)}, u32[]{:S(2)}, u32[]{:S(2)}) collective-permute-start(f32[18,8,256]{2,1,0:T(8,128)S(1)} %get-tuple-element.17), channel_id=1, source_target_pairs={{1,2},{3,4},{5,6},{7,8},{9,10},{11,12},{13,14},{15,16},{17,18},{19... | collective-permute-start | bytes 442376 | tf_op jit(solution)/shard_map/ppermute | solution.py:223
  20.2 8.0 %collective-permute-start.2 = (f32[18,8,256]{2,1,0:T(8,128)S(1)}, f32[18,8,256]{2,1,0:T(8,128)S(1)}, u32[]{:S(2)}, u32[]{:S(2)}) collective-permute-start(f32[18,8,256]{2,1,0:T(8,128)S(1)} %get-tuple-element.16.to_core), channel_id=1, source_target_pairs={{0,1},{2,3},{4,5},{6,7},{8,9},{10,11},{12,13},{14,15},{16,17},{18,... | collective-permute-start | bytes 442376 | tf_op jit(solution)/shard_map/ppermute | solution.py:223
  28.1 0.0 collective-permute-done.3.r_chip
  28.2 1.0 %collective-permute-done.2.r_core = f32[18,8,256]{2,1,0:T(8,128)S(1)} collective-permute-done((f32[18,8,256]{2,1,0:T(8,128)S(1)}, f32[18,8,256]{2,1,0:T(8,128)S(1)}, u32[]{:S(2)}, u32[]{:S(2)}) %collective-permute-start.2) | collective-permute-done | bytes 147488 | tf_op jit(solution)/shard_map/ppermute | solution.py:223
  29.1 1.0 %krylov.1 = (f32[4,16,24,256]{3,2,1,0:T(8,128)S(1)}, f32[32,1,128]{2,1,0:T(1,128)S(1)}) custom-call(s32[1]{0:T(128)} %bitcast.odd, f32[8,16,256]{2,1,0:T(8,128)S(1)} %get-tuple-element.11.t_own, f32[8,16,256]{2,1,0:T(8,128)S(1)} %get-tuple-element.12.d_own, f32[8,16,256]{2,1,0:T(8,128)S(1)} %get-tuple-element.13.scaling_own, ...), custom_call_target="tpu_custom_call" | custom-call | tf_op jit(solution)/shard_map/krylov/pallas_call | solution.py:267
  30.1 25.5 %all_to_all.10 = f32[32,1,128]{2,1,0:T(1,128)S(1)} all-to-all(f32[32,1,128]{2,1,0:T(1,128)S(1)} %get-tuple-element.18), channel_id=1, replica_groups=mesh['y'=8,'xh'=4,'xl'=2,'z'=8,'c'=2] {'xh','z'}, dimensions={0} | all-to-all | bytes 32768 | tf_op jit(solution)/shard_map/all_to_all | solution.py:227
  55.6 0.1 reduce_sum.9
  55.7 16.6 %all_to_all.11.parts = f32[32,1,128]{2,1,0:T(1,128)S(1)} all-to-all(f32[32,1,128]{2,1,0:T(1,128)S(1)} %broadcast_in_dim.2), channel_id=1, replica_groups=mesh['y'=8,'xh'=4,'xl'=2,'z'=8,'c'=2] {'y','xl','c'}, dimensions={0} | all-to-all | bytes 32768 | tf_op jit(solution)/shard_map/all_to_all | solution.py:279
  72.3 0.0 copy-done.1
  72.3 1.1 %finish.1 = (f32[3,8,16,256]{3,2,1,0:T(8,128)}, f32[8,16,256]{2,1,0:T(8,128)}) custom-call(f32[32,1,128]{2,1,0:T(1,128)S(1)} %all_to_all.11.parts, f32[4,16,24,256]{3,2,1,0:T(8,128)S(1)} %get-tuple-element.19.v, f32[3,8,16,256]{3,2,1,0:T(8,128)S(1)} %copy-done.1), custom_call_target="tpu_custom_call" | custom-call | tf_op jit(solution)/shard_map/finish/pallas_call | solution.py:281
  (2 shorter events, 0.0 us)
Async XLA Ops:
  0.6 1.0 %copy-start = (f32[3,8,16,256]{3,2,1,0:T(8,128)S(1)}, f32[3,8,16,256]{3,2,1,0:T(8,128)}, u32[]{:S(2)}) copy-start(f32[3,8,16,256]{3,2,1,0:T(8,128)} %cot.1) | copy-start | bytes 1179652
  1.6 0.9 %copy-start.2 = (f32[8,16,256]{2,1,0:T(8,128)S(1)}, f32[8,16,256]{2,1,0:T(8,128)}, u32[]{:S(2)}) copy-start(f32[8,16,256]{2,1,0:T(8,128)} %coef_hbm.1) | copy-start | bytes 393220
  2.5 69.8 %copy-start.1 = (f32[3,8,16,256]{3,2,1,0:T(8,128)S(1)}, f32[3,8,16,256]{3,2,1,0:T(8,128)}, u32[]{:S(2)}) copy-start(f32[3,8,16,256]{3,2,1,0:T(8,128)} %cot.1) | copy-start | bytes 1179652
  3.0 10.1 %collective-permute-start = (f32[10,16,256]{2,1,0:T(8,128)S(1)}, f32[10,16,256]{2,1,0:T(8,128)S(1)}, u32[]{:S(2)}, u32[]{:S(2)}) collective-permute-start(f32[10,16,256]{2,1,0:T(8,128)S(1)} %get-tuple-element.14.up), channel_id=1, source_target_pairs={{0,128},{1,129},{2,130},{3,131},{4,132},{5,133},{6,134},{7,135},{8... | collective-permute-start | bytes 491528 | tf_op jit(solution)/shard_map/ppermute | solution.py:218
  7.2 5.9 %collective-permute-start.1 = (f32[9,16,256]{2,1,0:T(8,128)S(1)}, f32[9,16,256]{2,1,0:T(8,128)S(1)}, u32[]{:S(2)}, u32[]{:S(2)}) collective-permute-start(f32[9,16,256]{2,1,0:T(8,128)S(1)} %get-tuple-element.15), channel_id=1, source_target_pairs={{128,0},{129,1},{130,2},{131,3},{132,4},{133,5},{134,6},{135,7},{1... | collective-permute-start | bytes 442376 | tf_op jit(solution)/shard_map/ppermute | solution.py:218
  13.1 15.0 %collective-permute-start.3 = (f32[18,8,256]{2,1,0:T(8,128)S(1)}, f32[18,8,256]{2,1,0:T(8,128)S(1)}, u32[]{:S(2)}, u32[]{:S(2)}) collective-permute-start(f32[18,8,256]{2,1,0:T(8,128)S(1)} %get-tuple-element.17), channel_id=1, source_target_pairs={{1,2},{3,4},{5,6},{7,8},{9,10},{11,12},{13,14},{15,16},{17,18},{19... | collective-permute-start | bytes 442376 | tf_op jit(solution)/shard_map/ppermute | solution.py:223
  20.2 9.0 %collective-permute-start.2 = (f32[18,8,256]{2,1,0:T(8,128)S(1)}, f32[18,8,256]{2,1,0:T(8,128)S(1)}, u32[]{:S(2)}, u32[]{:S(2)}) collective-permute-start(f32[18,8,256]{2,1,0:T(8,128)S(1)} %get-tuple-element.16.to_core), channel_id=1, source_target_pairs={{0,1},{2,3},{4,5},{6,7},{8,9},{10,11},{12,13},{14,15},{16,17},{18,... | collective-permute-start | bytes 442376 | tf_op jit(solution)/shard_map/ppermute | solution.py:223

commit v4 on v3

--- a/solution.py
+++ b/solution.py
@@ -14,7 +14,7 @@
 SPLIT = 0.6
 NMOM = 2 * ITERS
 AXES = ("y", "xh", "xl", "z", "c")
-STAGE = (("xh", "z"), ("y", "xl", "c"))
+STAGE = (("y", "xl", "c"), ("xh", "z"))
 F32 = jnp.float32
 
 
@@ -22,28 +22,18 @@
     return lax.broadcasted_iota(jnp.int32, shape, axis)
 
 
-def pack_kernel(cot_hbm, coef_hbm, t_out, d_out, scaling, up, down, cot, coef, sems):
-    copies = [
-        pltpu.make_async_copy(coef_hbm, coef, sems.at[0]),
-        pltpu.make_async_copy(cot_hbm, cot, sems.at[1]),
-    ]
-    for copy in copies:
-        copy.start()
-    for copy in copies:
-        copy.wait()
-    ny, nx, nz = coef.shape
+def pack_kernel(cot, scaling, t_out, d_out, up, down):
+    ny, nx, nz = scaling.shape
     sub, lane = iota((nx, nz), 0), iota((nx, nz), 1)
     column = jnp.zeros((nx, nz), F32)
     for y in range(ny):
         c0, c1, c2 = cot[0, y], cot[1, y], cot[2, y]
-        m = 6.0 + coef[y]
-        d = 1.0 / m
+        d = 1.0 / scaling[y]
         t = jnp.where(sub == 0, 0.0, pltpu.roll(c1, 1, 0)) - c1
         t = t + (jnp.where(lane == 0, 0.0, pltpu.roll(c2, 1, 1)) - c2)
         t = t + ((cot[0, y - 1] - c0) if y else -c0)
         t_out[y] = t
         d_out[y] = d
-        scaling[y] = m
         if y < HALO:
             down[y], down[HALO + y] = t, d
         if y >= ny - HALO:
@@ -236,18 +226,13 @@
 
     rows, wide = ny + 2 * HALO, nx + 8
     block = (ny, nx, nz)
-    t, d, scaling, up, down = pl.pallas_call(
+    scaling = 6.0 + coefficient
+    t, d, up, down = pl.pallas_call(
         pack_kernel,
-        in_specs=[pl.BlockSpec(memory_space=pltpu.HBM)] * 2,
-        out_shape=shapes(block, block, block, (2 * HALO + 2, nx, nz), (2 * HALO + 1, nx, nz)),
-        scratch_shapes=[
-            pltpu.VMEM(cotangent.shape, F32),
-            pltpu.VMEM(block, F32),
-            pltpu.SemaphoreType.DMA((2,)),
-        ],
+        out_shape=shapes(block, block, (2 * HALO + 2, nx, nz), (2 * HALO + 1, nx, nz)),
         compiler_params=limit,
         name="pack",
-    )(cotangent, coefficient)
+    )(cotangent, scaling)
     r_s = along_y(up, 1, gy, gx)
     r_n = along_y(down, -1, gy, gx)
     odd = lax.axis_index("c").astype(jnp.int32).reshape(1)

time: 73.7 us -> 72.3 us (0.981)
  blocking collectives: 42.1 us -> 41 us
  other arithmetic: 0.05 us -> 0.97 us
  local copies, waits for them, and re-layouts: 1.91 us -> 1.01 us
    all_to_all x1, blocking collectives: 25.5 us -> 21.4 us  [exchange_sum(): return jnp.sum(lax.all_to_all(x, axes, 0, 0), axis=0, keepdims=True)]
    all_to_all x1, blocking collectives: 16.6 us -> 19.7 us  [on_device(): lax.all_to_all(jnp.broadcast_to(part, (second, 1, 128)), STAGE[1], 0, 0)]
    add x0 -> x1, other arithmetic: none -> 0.92 us  [on_device(): scaling = 6.0 + coefficient]
    unnamed x6 -> x4, local copies, waits for them, and re-layouts: 1.9 us -> 0.99 us
where the time goes in v4:
time: 72.3 us; the launch traced here: 72 us
  blocking collectives  41 us (57%)
  starting transfers between devices  20.5 us (28%)
  waiting for transfers between devices  5.56 us (8%)
  Pallas kernels  2.24 us (3%)
  local copies, waits for them, and re-layouts  1.01 us (1%)
  other arithmetic  0.97 us (1%)
    all_to_all x1, blocking collectives, exchange_sum(): return jnp.sum(lax.all_to_all(x, axes, 0, 0), axis=0, keepdims=True)  21.4 us
    all_to_all x1, blocking collectives, on_device(): lax.all_to_all(jnp.broadcast_to(part, (second, 1, 128)), STAGE[1], 0, 0)  19.7 us
    ppermute x2, starting transfers between devices, pairs_along_x(): return lax.ppermute(x, AXES, up + [(j, i) for i, j in up])  15 us
    ppermute x2, starting transfers between devices, along_y(): lax.ppermute(x, AXES, [(a * nx + b, (a + dy) * nx + b) for a in range(ny)...  5.45 us
    ppermute x2, waiting for transfers between devices, along_y(): lax.ppermute(x, AXES, [(a * nx + b, (a + dy) * nx + b) for a in range(ny)...  4.59 us
  transfers between devices with their start and end apart: 4, of which 2 were waited for; matrix products, arithmetic and copies ran while one was open for 0% of the time, Pallas kernels for 0%

profile of v4, /device:TPU:1, one launch (start us, length us, event | category | flops | bytes accessed | tf_op | source)
XLA Modules:
  0.0 72.0 jit_solution(5697681558226805090)
XLA Ops:
  0.6 0.9 %broadcast_add_fusion.scaling.scaling_own = f32[8,16,256]{2,1,0:T(8,128)S(1)} fusion(f32[8,16,256]{2,1,0:T(8,128)} %param.3), kind=kLoop, calls=%fused_computation | loop fusion | flops 32768 | bytes 262144 | tf_op jit(solution)/shard_map/add | solution.py:229
  1.5 0.0 copy-start
  1.6 1.0 %copy-done = f32[3,8,16,256]{3,2,1,0:T(8,128)S(1)} copy-done((f32[3,8,16,256]{3,2,1,0:T(8,128)S(1)}, f32[3,8,16,256]{3,2,1,0:T(8,128)}, u32[]{:S(2)}) %copy-start) | copy-done | bytes 393240
  2.5 0.0 copy-start.1
  2.5 0.1 pack.1
  2.7 4.2 %collective-permute-start = (f32[10,16,256]{2,1,0:T(8,128)S(1)}, f32[10,16,256]{2,1,0:T(8,128)S(1)}, u32[]{:S(2)}, u32[]{:S(2)}) collective-permute-start(f32[10,16,256]{2,1,0:T(8,128)S(1)} %get-tuple-element.12.up), channel_id=1, source_target_pairs={{0,128},{1,129},{2,130},{3,131},{4,132},{5,133},{6,134},{7,135},{8... | collective-permute-start | bytes 491528 | tf_op jit(solution)/shard_map/ppermute | solution.py:208
  6.8 1.3 %collective-permute-start.1 = (f32[9,16,256]{2,1,0:T(8,128)S(1)}, f32[9,16,256]{2,1,0:T(8,128)S(1)}, u32[]{:S(2)}, u32[]{:S(2)}) collective-permute-start(f32[9,16,256]{2,1,0:T(8,128)S(1)} %get-tuple-element.13), channel_id=1, source_target_pairs={{128,0},{129,1},{130,2},{131,3},{132,4},{133,5},{134,6},{135,7},{1... | collective-permute-start | bytes 442376 | tf_op jit(solution)/shard_map/ppermute | solution.py:208
  8.1 4.6 %collective-permute-done.1.r_n = f32[9,16,256]{2,1,0:T(8,128)S(1)} collective-permute-done((f32[9,16,256]{2,1,0:T(8,128)S(1)}, f32[9,16,256]{2,1,0:T(8,128)S(1)}, u32[]{:S(2)}, u32[]{:S(2)}) %collective-permute-start.1) | collective-permute-done | bytes 147488 | tf_op jit(solution)/shard_map/ppermute | solution.py:208
  12.7 0.0 collective-permute-done.r_s
  12.7 7.1 %collective-permute-start.3 = (f32[18,8,256]{2,1,0:T(8,128)S(1)}, f32[18,8,256]{2,1,0:T(8,128)S(1)}, u32[]{:S(2)}, u32[]{:S(2)}) collective-permute-start(f32[18,8,256]{2,1,0:T(8,128)S(1)} %get-tuple-element.15), channel_id=1, source_target_pairs={{1,2},{3,4},{5,6},{7,8},{9,10},{11,12},{13,14},{15,16},{17,18},{19... | collective-permute-start | bytes 442376 | tf_op jit(solution)/shard_map/ppermute | solution.py:213
  19.8 8.0 %collective-permute-start.2 = (f32[18,8,256]{2,1,0:T(8,128)S(1)}, f32[18,8,256]{2,1,0:T(8,128)S(1)}, u32[]{:S(2)}, u32[]{:S(2)}) collective-permute-start(f32[18,8,256]{2,1,0:T(8,128)S(1)} %get-tuple-element.14.to_core), channel_id=1, source_target_pairs={{0,1},{2,3},{4,5},{6,7},{8,9},{10,11},{12,13},{14,15},{16,17},{18,... | collective-permute-start | bytes 442376 | tf_op jit(solution)/shard_map/ppermute | solution.py:213
  27.8 0.0 collective-permute-done.3.r_chip
  27.8 1.0 %collective-permute-done.2.r_core = f32[18,8,256]{2,1,0:T(8,128)S(1)} collective-permute-done((f32[18,8,256]{2,1,0:T(8,128)S(1)}, f32[18,8,256]{2,1,0:T(8,128)S(1)}, u32[]{:S(2)}, u32[]{:S(2)}) %collective-permute-start.2) | collective-permute-done | bytes 147488 | tf_op jit(solution)/shard_map/ppermute | solution.py:213
  28.8 1.0 %krylov.1 = (f32[4,16,24,256]{3,2,1,0:T(8,128)S(1)}, f32[32,1,128]{2,1,0:T(1,128)S(1)}) custom-call(s32[1]{0:T(128)} %bitcast.odd, f32[8,16,256]{2,1,0:T(8,128)S(1)} %get-tuple-element.10.t_own, f32[8,16,256]{2,1,0:T(8,128)S(1)} %get-tuple-element.11.d_own, f32[8,16,256]{2,1,0:T(8,128)S(1)} %broadcast_add_fusion.scaling.scaling_own, ...), custom_call_target="tpu_custom_call" | custom-call | tf_op jit(solution)/shard_map/krylov/pallas_call | solution.py:252
  29.8 21.4 %all_to_all.10 = f32[32,1,128]{2,1,0:T(1,128)S(1)} all-to-all(f32[32,1,128]{2,1,0:T(1,128)S(1)} %get-tuple-element.16), channel_id=1, replica_groups=mesh['y'=8,'xh'=4,'xl'=2,'z'=8,'c'=2] {'y','xl','c'}, dimensions={0} | all-to-all | bytes 32768 | tf_op jit(solution)/shard_map/all_to_all | solution.py:217
  51.2 0.1 reduce_sum.9
  51.2 19.7 %all_to_all.11.parts = f32[32,1,128]{2,1,0:T(1,128)S(1)} all-to-all(f32[32,1,128]{2,1,0:T(1,128)S(1)} %broadcast_in_dim.2), channel_id=1, replica_groups=mesh['y'=8,'xh'=4,'xl'=2,'z'=8,'c'=2] {'xh','z'}, dimensions={0} | all-to-all | bytes 32768 | tf_op jit(solution)/shard_map/all_to_all | solution.py:264
  70.9 0.0 copy-done.1
  70.9 1.1 %finish.1 = (f32[3,8,16,256]{3,2,1,0:T(8,128)}, f32[8,16,256]{2,1,0:T(8,128)}) custom-call(f32[32,1,128]{2,1,0:T(1,128)S(1)} %all_to_all.11.parts, f32[4,16,24,256]{3,2,1,0:T(8,128)S(1)} %get-tuple-element.17.v, f32[3,8,16,256]{3,2,1,0:T(8,128)S(1)} %copy-done.1), custom_call_target="tpu_custom_call" | custom-call | tf_op jit(solution)/shard_map/finish/pallas_call | solution.py:266
  (2 shorter events, 0.0 us)
Async XLA Ops:
  1.5 1.0 %copy-start = (f32[3,8,16,256]{3,2,1,0:T(8,128)S(1)}, f32[3,8,16,256]{3,2,1,0:T(8,128)}, u32[]{:S(2)}) copy-start(f32[3,8,16,256]{3,2,1,0:T(8,128)} %cot.3) | copy-start | bytes 1179652
  2.5 68.4 %copy-start.1 = (f32[3,8,16,256]{3,2,1,0:T(8,128)S(1)}, f32[3,8,16,256]{3,2,1,0:T(8,128)}, u32[]{:S(2)}) copy-start(f32[3,8,16,256]{3,2,1,0:T(8,128)} %cot.3) | copy-start | bytes 1179652
  2.7 10.1 %collective-permute-start = (f32[10,16,256]{2,1,0:T(8,128)S(1)}, f32[10,16,256]{2,1,0:T(8,128)S(1)}, u32[]{:S(2)}, u32[]{:S(2)}) collective-permute-start(f32[10,16,256]{2,1,0:T(8,128)S(1)} %get-tuple-element.12.up), channel_id=1, source_target_pairs={{0,128},{1,129},{2,130},{3,131},{4,132},{5,133},{6,134},{7,135},{8... | collective-permute-start | bytes 491528 | tf_op jit(solution)/shard_map/ppermute | solution.py:208
  6.8 5.9 %collective-permute-start.1 = (f32[9,16,256]{2,1,0:T(8,128)S(1)}, f32[9,16,256]{2,1,0:T(8,128)S(1)}, u32[]{:S(2)}, u32[]{:S(2)}) collective-permute-start(f32[9,16,256]{2,1,0:T(8,128)S(1)} %get-tuple-element.13), channel_id=1, source_target_pairs={{128,0},{129,1},{130,2},{131,3},{132,4},{133,5},{134,6},{135,7},{1... | collective-permute-start | bytes 442376 | tf_op jit(solution)/shard_map/ppermute | solution.py:208
  12.7 15.0 %collective-permute-start.3 = (f32[18,8,256]{2,1,0:T(8,128)S(1)}, f32[18,8,256]{2,1,0:T(8,128)S(1)}, u32[]{:S(2)}, u32[]{:S(2)}) collective-permute-start(f32[18,8,256]{2,1,0:T(8,128)S(1)} %get-tuple-element.15), channel_id=1, source_target_pairs={{1,2},{3,4},{5,6},{7,8},{9,10},{11,12},{13,14},{15,16},{17,18},{19... | collective-permute-start | bytes 442376 | tf_op jit(solution)/shard_map/ppermute | solution.py:213
  19.8 9.0 %collective-permute-start.2 = (f32[18,8,256]{2,1,0:T(8,128)S(1)}, f32[18,8,256]{2,1,0:T(8,128)S(1)}, u32[]{:S(2)}, u32[]{:S(2)}) collective-permute-start(f32[18,8,256]{2,1,0:T(8,128)S(1)} %get-tuple-element.14.to_core), channel_id=1, source_target_pairs={{0,1},{2,3},{4,5},{6,7},{8,9},{10,11},{12,13},{14,15},{16,17},{18,... | collective-permute-start | bytes 442376 | tf_op jit(solution)/shard_map/ppermute | solution.py:213

commit v5 on v4

--- a/solution.py
+++ b/solution.py
@@ -22,16 +22,18 @@
     return lax.broadcasted_iota(jnp.int32, shape, axis)
 
 
-def pack_kernel(cot, scaling, t_out, d_out, up, down):
-    ny, nx, nz = scaling.shape
+def pack_kernel(fields, t_out, d_out, scaling, up, down):
+    ny, nx, nz = t_out.shape
     sub, lane = iota((nx, nz), 0), iota((nx, nz), 1)
     column = jnp.zeros((nx, nz), F32)
     for y in range(ny):
-        c0, c1, c2 = cot[0, y], cot[1, y], cot[2, y]
-        d = 1.0 / scaling[y]
+        c0, c1, c2 = fields[0, y], fields[1, y], fields[2, y]
+        m = 6.0 + fields[3, y]
+        d = 1.0 / m
+        scaling[y] = m
         t = jnp.where(sub == 0, 0.0, pltpu.roll(c1, 1, 0)) - c1
         t = t + (jnp.where(lane == 0, 0.0, pltpu.roll(c2, 1, 1)) - c2)
-        t = t + ((cot[0, y - 1] - c0) if y else -c0)
+        t = t + ((fields[0, y - 1] - c0) if y else -c0)
         t_out[y] = t
         d_out[y] = d
         if y < HALO:
@@ -40,7 +42,7 @@
             j = y - (ny - HALO)
             up[j], up[HALO + j] = t, d
         column = jnp.where(sub == y, jnp.broadcast_to(c1[nx - 1 : nx], (nx, nz)), column)
-    up[2 * HALO] = cot[0, ny - 1]
+    up[2 * HALO] = fields[0, ny - 1]
     up[2 * HALO + 1] = column
     down[2 * HALO] = column
 
@@ -177,7 +179,7 @@
 
 
 def finish_kernel(parts, v, cot, vel, adj):
-    _, ny, nx, nz = cot.shape
+    ny, nx, nz = adj.shape
     line = jnp.sum(parts[...], axis=0)
     spread = jnp.broadcast_to(line, (8, 128))
     lane = iota((8, 128), 1)
@@ -226,13 +228,13 @@
 
     rows, wide = ny + 2 * HALO, nx + 8
     block = (ny, nx, nz)
-    scaling = 6.0 + coefficient
-    t, d, up, down = pl.pallas_call(
+    fields = jnp.concatenate([cotangent, coefficient[None]], axis=0)
+    t, d, scaling, up, down = pl.pallas_call(
         pack_kernel,
-        out_shape=shapes(block, block, (2 * HALO + 2, nx, nz), (2 * HALO + 1, nx, nz)),
+        out_shape=shapes(block, block, block, (2 * HALO + 2, nx, nz), (2 * HALO + 1, nx, nz)),
         compiler_params=limit,
         name="pack",
-    )(cotangent, scaling)
+    )(fields)
     r_s = along_y(up, 1, gy, gx)
     r_n = along_y(down, -1, gy, gx)
     odd = lax.axis_index("c").astype(jnp.int32).reshape(1)
@@ -271,7 +273,7 @@
             ],
             compiler_params=limit,
             name="finish",
-        )(part, v, cotangent)
+        )(part, v, fields)
     )
 
 

time: 72.3 us -> 71.5 us (0.989)
  local copies, waits for them, and re-layouts: 1.01 us -> 0.01 us
    concatenate x0 -> x1, other arithmetic: none -> 1.1 us  [on_device(): fields = jnp.concatenate([cotangent, coefficient[None]], axis=0)]
    unnamed x4 -> x0, local copies, waits for them, and re-layouts: 0.99 us -> none
    add x1 -> x0, other arithmetic: 0.92 us -> none  [on_device(): scaling = 6.0 + coefficient]
where the time goes in v5:
time: 71.5 us; the launch traced here: 71.2 us
  blocking collectives  41 us (57%)
  starting transfers between devices  20.5 us (29%)
  waiting for transfers between devices  5.56 us (8%)
  Pallas kernels  2.24 us (3%)
  other arithmetic  1.15 us (2%)
    all_to_all x1, blocking collectives, exchange_sum(): return jnp.sum(lax.all_to_all(x, axes, 0, 0), axis=0, keepdims=True)  21.4 us
    all_to_all x1, blocking collectives, on_device(): lax.all_to_all(jnp.broadcast_to(part, (second, 1, 128)), STAGE[1], 0, 0)  19.7 us
    ppermute x2, starting transfers between devices, pairs_along_x(): return lax.ppermute(x, AXES, up + [(j, i) for i, j in up])  15 us
    ppermute x2, starting transfers between devices, along_y(): lax.ppermute(x, AXES, [(a * nx + b, (a + dy) * nx + b) for a in range(ny)...  5.45 us
    ppermute x2, waiting for transfers between devices, along_y(): lax.ppermute(x, AXES, [(a * nx + b, (a + dy) * nx + b) for a in range(ny)...  4.59 us
  transfers between devices with their start and end apart: 4, of which 2 were waited for; matrix products, arithmetic and copies ran while one was open for 0% of the time, Pallas kernels for 0%

profile of v5, /device:TPU:1, one launch (start us, length us, event | category | flops | bytes accessed | tf_op | source)
XLA Modules:
  0.0 71.2 jit_solution(18282590415985611857)
XLA Ops:
  0.6 1.1 %pad_maximum_fusion.fields.cot = f32[4,8,16,256]{3,2,1,0:T(8,128)S(1)} fusion(f32[1,8,16,256]{3,2,1,0:T(8,128)} %bitcast.2, f32[3,8,16,256]{3,2,1,0:T(8,128)} %param.2), kind=kLoop, calls=%fused_computation | loop fusion | flops 131072 | bytes 1048576 | tf_op jit(solution)/shard_map/concatenate | solution.py:231
  1.7 0.1 pack.1
  1.8 4.2 %collective-permute-start = (f32[10,16,256]{2,1,0:T(8,128)S(1)}, f32[10,16,256]{2,1,0:T(8,128)S(1)}, u32[]{:S(2)}, u32[]{:S(2)}) collective-permute-start(f32[10,16,256]{2,1,0:T(8,128)S(1)} %get-tuple-element.14.up), channel_id=1, source_target_pairs={{0,128},{1,129},{2,130},{3,131},{4,132},{5,133},{6,134},{7,135},{8... | collective-permute-start | bytes 491528 | tf_op jit(solution)/shard_map/ppermute | solution.py:210
  6.0 1.3 %collective-permute-start.1 = (f32[9,16,256]{2,1,0:T(8,128)S(1)}, f32[9,16,256]{2,1,0:T(8,128)S(1)}, u32[]{:S(2)}, u32[]{:S(2)}) collective-permute-start(f32[9,16,256]{2,1,0:T(8,128)S(1)} %get-tuple-element.15), channel_id=1, source_target_pairs={{128,0},{129,1},{130,2},{131,3},{132,4},{133,5},{134,6},{135,7},{1... | collective-permute-start | bytes 442376 | tf_op jit(solution)/shard_map/ppermute | solution.py:210
  7.3 4.6 %collective-permute-done.1.r_n = f32[9,16,256]{2,1,0:T(8,128)S(1)} collective-permute-done((f32[9,16,256]{2,1,0:T(8,128)S(1)}, f32[9,16,256]{2,1,0:T(8,128)S(1)}, u32[]{:S(2)}, u32[]{:S(2)}) %collective-permute-start.1) | collective-permute-done | bytes 147488 | tf_op jit(solution)/shard_map/ppermute | solution.py:210
  11.9 0.0 collective-permute-done.r_s
  11.9 7.1 %collective-permute-start.3 = (f32[18,8,256]{2,1,0:T(8,128)S(1)}, f32[18,8,256]{2,1,0:T(8,128)S(1)}, u32[]{:S(2)}, u32[]{:S(2)}) collective-permute-start(f32[18,8,256]{2,1,0:T(8,128)S(1)} %get-tuple-element.17), channel_id=1, source_target_pairs={{1,2},{3,4},{5,6},{7,8},{9,10},{11,12},{13,14},{15,16},{17,18},{19... | collective-permute-start | bytes 442376 | tf_op jit(solution)/shard_map/ppermute | solution.py:215
  19.0 8.0 %collective-permute-start.2 = (f32[18,8,256]{2,1,0:T(8,128)S(1)}, f32[18,8,256]{2,1,0:T(8,128)S(1)}, u32[]{:S(2)}, u32[]{:S(2)}) collective-permute-start(f32[18,8,256]{2,1,0:T(8,128)S(1)} %get-tuple-element.16.to_core), channel_id=1, source_target_pairs={{0,1},{2,3},{4,5},{6,7},{8,9},{10,11},{12,13},{14,15},{16,17},{18,... | collective-permute-start | bytes 442376 | tf_op jit(solution)/shard_map/ppermute | solution.py:215
  27.0 0.0 collective-permute-done.3.r_chip
  27.0 1.0 %collective-permute-done.2.r_core = f32[18,8,256]{2,1,0:T(8,128)S(1)} collective-permute-done((f32[18,8,256]{2,1,0:T(8,128)S(1)}, f32[18,8,256]{2,1,0:T(8,128)S(1)}, u32[]{:S(2)}, u32[]{:S(2)}) %collective-permute-start.2) | collective-permute-done | bytes 147488 | tf_op jit(solution)/shard_map/ppermute | solution.py:215
  28.0 1.0 %krylov.1 = (f32[4,16,24,256]{3,2,1,0:T(8,128)S(1)}, f32[32,1,128]{2,1,0:T(1,128)S(1)}) custom-call(s32[1]{0:T(128)} %bitcast.odd, f32[8,16,256]{2,1,0:T(8,128)S(1)} %get-tuple-element.11.t_own, f32[8,16,256]{2,1,0:T(8,128)S(1)} %get-tuple-element.12.d_own, f32[8,16,256]{2,1,0:T(8,128)S(1)} %get-tuple-element.13.scaling_own, ...), custom_call_target="tpu_custom_call" | custom-call | tf_op jit(solution)/shard_map/krylov/pallas_call | solution.py:254
  29.0 21.4 %all_to_all.10 = f32[32,1,128]{2,1,0:T(1,128)S(1)} all-to-all(f32[32,1,128]{2,1,0:T(1,128)S(1)} %get-tuple-element.18), channel_id=1, replica_groups=mesh['y'=8,'xh'=4,'xl'=2,'z'=8,'c'=2] {'y','xl','c'}, dimensions={0} | all-to-all | bytes 32768 | tf_op jit(solution)/shard_map/all_to_all | solution.py:219
  50.4 0.1 reduce_sum.9
  50.4 19.7 %all_to_all.11.parts = f32[32,1,128]{2,1,0:T(1,128)S(1)} all-to-all(f32[32,1,128]{2,1,0:T(1,128)S(1)} %broadcast_in_dim.10), channel_id=1, replica_groups=mesh['y'=8,'xh'=4,'xl'=2,'z'=8,'c'=2] {'xh','z'}, dimensions={0} | all-to-all | bytes 32768 | tf_op jit(solution)/shard_map/all_to_all | solution.py:266
  70.1 1.1 %finish.1 = (f32[3,8,16,256]{3,2,1,0:T(8,128)}, f32[8,16,256]{2,1,0:T(8,128)}) custom-call(f32[32,1,128]{2,1,0:T(1,128)S(1)} %all_to_all.11.parts, f32[4,16,24,256]{3,2,1,0:T(8,128)S(1)} %get-tuple-element.19.v, f32[4,8,16,256]{3,2,1,0:T(8,128)S(1)} %pad_maximum_fusion.fields.cot), custom_call_target="tpu_custom_call" | custom-call | tf_op jit(solution)/shard_map/finish/pallas_call | solution.py:268
  (2 shorter events, 0.0 us)
Async XLA Ops:
  1.8 10.1 %collective-permute-start = (f32[10,16,256]{2,1,0:T(8,128)S(1)}, f32[10,16,256]{2,1,0:T(8,128)S(1)}, u32[]{:S(2)}, u32[]{:S(2)}) collective-permute-start(f32[10,16,256]{2,1,0:T(8,128)S(1)} %get-tuple-element.14.up), channel_id=1, source_target_pairs={{0,128},{1,129},{2,130},{3,131},{4,132},{5,133},{6,134},{7,135},{8... | collective-permute-start | bytes 491528 | tf_op jit(solution)/shard_map/ppermute | solution.py:210
  6.0 5.9 %collective-permute-start.1 = (f32[9,16,256]{2,1,0:T(8,128)S(1)}, f32[9,16,256]{2,1,0:T(8,128)S(1)}, u32[]{:S(2)}, u32[]{:S(2)}) collective-permute-start(f32[9,16,256]{2,1,0:T(8,128)S(1)} %get-tuple-element.15), channel_id=1, source_target_pairs={{128,0},{129,1},{130,2},{131,3},{132,4},{133,5},{134,6},{135,7},{1... | collective-permute-start | bytes 442376 | tf_op jit(solution)/shard_map/ppermute | solution.py:210
  11.9 15.0 %collective-permute-start.3 = (f32[18,8,256]{2,1,0:T(8,128)S(1)}, f32[18,8,256]{2,1,0:T(8,128)S(1)}, u32[]{:S(2)}, u32[]{:S(2)}) collective-permute-start(f32[18,8,256]{2,1,0:T(8,128)S(1)} %get-tuple-element.17), channel_id=1, source_target_pairs={{1,2},{3,4},{5,6},{7,8},{9,10},{11,12},{13,14},{15,16},{17,18},{19... | collective-permute-start | bytes 442376 | tf_op jit(solution)/shard_map/ppermute | solution.py:215
  19.0 9.0 %collective-permute-start.2 = (f32[18,8,256]{2,1,0:T(8,128)S(1)}, f32[18,8,256]{2,1,0:T(8,128)S(1)}, u32[]{:S(2)}, u32[]{:S(2)}) collective-permute-start(f32[18,8,256]{2,1,0:T(8,128)S(1)} %get-tuple-element.16.to_core), channel_id=1, source_target_pairs={{0,1},{2,3},{4,5},{6,7},{8,9},{10,11},{12,13},{14,15},{16,17},{18,... | collective-permute-start | bytes 442376 | tf_op jit(solution)/shard_map/ppermute | solution.py:215

commit v6 on v5

--- a/solution.py
+++ b/solution.py
@@ -59,16 +59,21 @@
     return out + [(r_s[j], r_s[HALO + j]) for j in range(HALO)]
 
 
+def sent_along_x(ny):
+    return [row for row in range(ny + 2 * HALO) if row not in (ny + HALO - 1, ny + HALO)]
+
+
 def side_kernel(odd, t_own, d_own, up, r_s, r_n, to_core, to_chip):
     ny, nx, nz = t_own.shape
     low = iota((8, nz), 0) < 4
     even = odd[0] == 0
-    for row, (t, d) in enumerate(window_rows(t_own, d_own, up, r_s, r_n)):
+    window = window_rows(t_own, d_own, up, r_s, r_n)
+    for row, (t, d) in enumerate(window[k] for k in sent_along_x(ny)):
         right = jnp.where(low, pltpu.roll(d[nx - 8 :], 4, 0), t[nx - 8 :])
         left = jnp.where(low, t[:8], pltpu.roll(d[:8], 4, 0))
         to_core[row] = jnp.where(even, right, left)
         to_chip[row] = jnp.where(even, left, right)
-    rows = ny + 2 * HALO
+    rows = ny + 2 * HALO - 2
     for to in (to_core, to_chip):
         to[rows] = up[2 * HALO + 1, :8]
         to[rows + 1] = jnp.where(low, r_n[2 * HALO, :8], r_s[2 * HALO + 1, :8])
@@ -87,7 +92,8 @@
     def from_right(row):
         return jnp.where(even, r_core[row], r_chip[row])
 
-    columns = [(from_left(ny + 2 * HALO + i), to_core[ny + 2 * HALO + i]) for i in range(2)]
+    sent = sent_along_x(ny)
+    columns = [(from_left(len(sent) + i), to_core[len(sent) + i]) for i in range(2)]
 
     def at_first(column, k):
         return jnp.where(sub8 == 0, jnp.broadcast_to(column[k : k + 1], (8, nz)), 0.0)
@@ -96,11 +102,15 @@
         before, after = columns[row // 8]
         v[0, row, 0:8] = (t[:8] + at_first(before, row % 8)) * d[:8]
         v[0, row, 8:nx] = t[8:] * d[8:]
-        left, right = from_left(row), from_right(row)
+        dw[row, 0:nx] = d
+        if row not in sent:
+            v[0, row, nx : nx + 8] = jnp.zeros((8, nz), F32)
+            dw[row, nx : nx + 8] = jnp.zeros((8, nz), F32)
+            continue
+        left, right = from_left(sent.index(row)), from_right(sent.index(row))
         t = jnp.where(low, right, left) + at_first(after, row % 8)
         d_side = pltpu.roll(jnp.where(low, left, right), 4, 0)
         v[0, row, nx : nx + 8] = t * d_side
-        dw[row, 0:nx] = d
         dw[row, nx : nx + 8] = d_side
 
     rows = ny + 2 * HALO
@@ -240,7 +250,7 @@
     odd = lax.axis_index("c").astype(jnp.int32).reshape(1)
     scalar = pl.BlockSpec(memory_space=pltpu.SMEM)
     whole = pl.BlockSpec(memory_space=pltpu.VMEM)
-    side = (rows + 2, 8, nz)
+    side = (rows, 8, nz)
     to_core, to_chip = pl.pallas_call(
         side_kernel,
         in_specs=[scalar] + [whole] * 5,

time: 71.5 us -> 71.3 us (level)
  no operation moved by 1% of the time
where the time goes in v6:
time: 71.3 us; the launch traced here: 71 us
  blocking collectives  40.9 us (57%)
  starting transfers between devices  20.5 us (29%)
  waiting for transfers between devices  5.54 us (8%)
  Pallas kernels  2.23 us (3%)
  other arithmetic  1.15 us (2%)
    all_to_all x1, blocking collectives, exchange_sum(): return jnp.sum(lax.all_to_all(x, axes, 0, 0), axis=0, keepdims=True)  21.4 us
    all_to_all x1, blocking collectives, on_device(): lax.all_to_all(jnp.broadcast_to(part, (second, 1, 128)), STAGE[1], 0, 0)  19.5 us
    ppermute x2, starting transfers between devices, pairs_along_x(): return lax.ppermute(x, AXES, up + [(j, i) for i, j in up])  15 us
    ppermute x2, starting transfers between devices, along_y(): lax.ppermute(x, AXES, [(a * nx + b, (a + dy) * nx + b) for a in range(ny)...  5.45 us
    ppermute x2, waiting for transfers between devices, along_y(): lax.ppermute(x, AXES, [(a * nx + b, (a + dy) * nx + b) for a in range(ny)...  4.59 us
  transfers between devices with their start and end apart: 4, of which 2 were waited for; matrix products, arithmetic and copies ran while one was open for 0% of the time, Pallas kernels for 0%

profile of v6, /device:TPU:1, one launch (start us, length us, event | category | flops | bytes accessed | tf_op | source)
XLA Modules:
  0.0 71.0 jit_solution(8608178631778892441)
XLA Ops:
  0.6 1.1 %pad_maximum_fusion.fields.cot = f32[4,8,16,256]{3,2,1,0:T(8,128)S(1)} fusion(f32[1,8,16,256]{3,2,1,0:T(8,128)} %bitcast.2, f32[3,8,16,256]{3,2,1,0:T(8,128)} %param.2), kind=kLoop, calls=%fused_computation | loop fusion | flops 131072 | bytes 1048576 | tf_op jit(solution)/shard_map/concatenate | solution.py:241
  1.7 0.1 pack.1
  1.8 4.2 %collective-permute-start = (f32[10,16,256]{2,1,0:T(8,128)S(1)}, f32[10,16,256]{2,1,0:T(8,128)S(1)}, u32[]{:S(2)}, u32[]{:S(2)}) collective-permute-start(f32[10,16,256]{2,1,0:T(8,128)S(1)} %get-tuple-element.14.up), channel_id=1, source_target_pairs={{0,128},{1,129},{2,130},{3,131},{4,132},{5,133},{6,134},{7,135},{8... | collective-permute-start | bytes 491528 | tf_op jit(solution)/shard_map/ppermute | solution.py:220
  6.0 1.3 %collective-permute-start.1 = (f32[9,16,256]{2,1,0:T(8,128)S(1)}, f32[9,16,256]{2,1,0:T(8,128)S(1)}, u32[]{:S(2)}, u32[]{:S(2)}) collective-permute-start(f32[9,16,256]{2,1,0:T(8,128)S(1)} %get-tuple-element.15), channel_id=1, source_target_pairs={{128,0},{129,1},{130,2},{131,3},{132,4},{133,5},{134,6},{135,7},{1... | collective-permute-start | bytes 442376 | tf_op jit(solution)/shard_map/ppermute | solution.py:220
  7.3 4.6 %collective-permute-done.1.r_n = f32[9,16,256]{2,1,0:T(8,128)S(1)} collective-permute-done((f32[9,16,256]{2,1,0:T(8,128)S(1)}, f32[9,16,256]{2,1,0:T(8,128)S(1)}, u32[]{:S(2)}, u32[]{:S(2)}) %collective-permute-start.1) | collective-permute-done | bytes 147488 | tf_op jit(solution)/shard_map/ppermute | solution.py:220
  11.9 0.0 collective-permute-done.r_s
  11.9 7.1 %collective-permute-start.3 = (f32[16,8,256]{2,1,0:T(8,128)S(1)}, f32[16,8,256]{2,1,0:T(8,128)S(1)}, u32[]{:S(2)}, u32[]{:S(2)}) collective-permute-start(f32[16,8,256]{2,1,0:T(8,128)S(1)} %get-tuple-element.17), channel_id=1, source_target_pairs={{1,2},{3,4},{5,6},{7,8},{9,10},{11,12},{13,14},{15,16},{17,18},{19... | collective-permute-start | bytes 393224 | tf_op jit(solution)/shard_map/ppermute | solution.py:225
  19.0 8.0 %collective-permute-start.2 = (f32[16,8,256]{2,1,0:T(8,128)S(1)}, f32[16,8,256]{2,1,0:T(8,128)S(1)}, u32[]{:S(2)}, u32[]{:S(2)}) collective-permute-start(f32[16,8,256]{2,1,0:T(8,128)S(1)} %get-tuple-element.16.to_core), channel_id=1, source_target_pairs={{0,1},{2,3},{4,5},{6,7},{8,9},{10,11},{12,13},{14,15},{16,17},{18,... | collective-permute-start | bytes 393224 | tf_op jit(solution)/shard_map/ppermute | solution.py:225
  27.0 0.0 collective-permute-done.3.r_chip
  27.0 1.0 %collective-permute-done.2.r_core = f32[16,8,256]{2,1,0:T(8,128)S(1)} collective-permute-done((f32[16,8,256]{2,1,0:T(8,128)S(1)}, f32[16,8,256]{2,1,0:T(8,128)S(1)}, u32[]{:S(2)}, u32[]{:S(2)}) %collective-permute-start.2) | collective-permute-done | bytes 131104 | tf_op jit(solution)/shard_map/ppermute | solution.py:225
  27.9 1.0 %krylov.1 = (f32[4,16,24,256]{3,2,1,0:T(8,128)S(1)}, f32[32,1,128]{2,1,0:T(1,128)S(1)}) custom-call(s32[1]{0:T(128)} %bitcast.odd, f32[8,16,256]{2,1,0:T(8,128)S(1)} %get-tuple-element.11.t_own, f32[8,16,256]{2,1,0:T(8,128)S(1)} %get-tuple-element.12.d_own, f32[8,16,256]{2,1,0:T(8,128)S(1)} %get-tuple-element.13.scaling_own, ...), custom_call_target="tpu_custom_call" | custom-call | tf_op jit(solution)/shard_map/krylov/pallas_call | solution.py:264
  29.0 21.4 %all_to_all.10 = f32[32,1,128]{2,1,0:T(1,128)S(1)} all-to-all(f32[32,1,128]{2,1,0:T(1,128)S(1)} %get-tuple-element.18), channel_id=1, replica_groups=mesh['y'=8,'xh'=4,'xl'=2,'z'=8,'c'=2] {'y','xl','c'}, dimensions={0} | all-to-all | bytes 32768 | tf_op jit(solution)/shard_map/all_to_all | solution.py:229
  50.3 0.1 reduce_sum.9
  50.4 19.5 %all_to_all.11.parts = f32[32,1,128]{2,1,0:T(1,128)S(1)} all-to-all(f32[32,1,128]{2,1,0:T(1,128)S(1)} %broadcast_in_dim.10), channel_id=1, replica_groups=mesh['y'=8,'xh'=4,'xl'=2,'z'=8,'c'=2] {'xh','z'}, dimensions={0} | all-to-all | bytes 32768 | tf_op jit(solution)/shard_map/all_to_all | solution.py:276
  69.9 1.1 %finish.1 = (f32[3,8,16,256]{3,2,1,0:T(8,128)}, f32[8,16,256]{2,1,0:T(8,128)}) custom-call(f32[32,1,128]{2,1,0:T(1,128)S(1)} %all_to_all.11.parts, f32[4,16,24,256]{3,2,1,0:T(8,128)S(1)} %get-tuple-element.19.v, f32[4,8,16,256]{3,2,1,0:T(8,128)S(1)} %pad_maximum_fusion.fields.cot), custom_call_target="tpu_custom_call" | custom-call | tf_op jit(solution)/shard_map/finish/pallas_call | solution.py:278
  (2 shorter events, 0.0 us)
Async XLA Ops:
  1.8 10.1 %collective-permute-start = (f32[10,16,256]{2,1,0:T(8,128)S(1)}, f32[10,16,256]{2,1,0:T(8,128)S(1)}, u32[]{:S(2)}, u32[]{:S(2)}) collective-permute-start(f32[10,16,256]{2,1,0:T(8,128)S(1)} %get-tuple-element.14.up), channel_id=1, source_target_pairs={{0,128},{1,129},{2,130},{3,131},{4,132},{5,133},{6,134},{7,135},{8... | collective-permute-start | bytes 491528 | tf_op jit(solution)/shard_map/ppermute | solution.py:220
  6.0 5.9 %collective-permute-start.1 = (f32[9,16,256]{2,1,0:T(8,128)S(1)}, f32[9,16,256]{2,1,0:T(8,128)S(1)}, u32[]{:S(2)}, u32[]{:S(2)}) collective-permute-start(f32[9,16,256]{2,1,0:T(8,128)S(1)} %get-tuple-element.15), channel_id=1, source_target_pairs={{128,0},{129,1},{130,2},{131,3},{132,4},{133,5},{134,6},{135,7},{1... | collective-permute-start | bytes 442376 | tf_op jit(solution)/shard_map/ppermute | solution.py:220
  11.9 15.0 %collective-permute-start.3 = (f32[16,8,256]{2,1,0:T(8,128)S(1)}, f32[16,8,256]{2,1,0:T(8,128)S(1)}, u32[]{:S(2)}, u32[]{:S(2)}) collective-permute-start(f32[16,8,256]{2,1,0:T(8,128)S(1)} %get-tuple-element.17), channel_id=1, source_target_pairs={{1,2},{3,4},{5,6},{7,8},{9,10},{11,12},{13,14},{15,16},{17,18},{19... | collective-permute-start | bytes 393224 | tf_op jit(solution)/shard_map/ppermute | solution.py:225
  19.0 8.9 %collective-permute-start.2 = (f32[16,8,256]{2,1,0:T(8,128)S(1)}, f32[16,8,256]{2,1,0:T(8,128)S(1)}, u32[]{:S(2)}, u32[]{:S(2)}) collective-permute-start(f32[16,8,256]{2,1,0:T(8,128)S(1)} %get-tuple-element.16.to_core), channel_id=1, source_target_pairs={{0,1},{2,3},{4,5},{6,7},{8,9},{10,11},{12,13},{14,15},{16,17},{18,... | collective-permute-start | bytes 393224 | tf_op jit(solution)/shard_map/ppermute | solution.py:225
